TPU v7x, 32 devices: a whole 2x2x4 slice. The times are simulated.
32 devices in a mesh: gx: 8 (over z, core), gy: 4 (over y, x).
Axes of the slice: x: 2, y: 2, z: 4, core: 2. Of those that a mesh axis runs over, the one named last changes fastest.
Arguments:
- prev_wave: float32 [32, 256, 2048], P(None, 'gy', 'gx'), may hold values from -6 to 6
- source: float32 [32, 256, 2048], P(None, 'gy', 'gx'), may hold values from -6 to 6
- start_state: float32 [256, 2048], P('gy', 'gx'), may hold values from -6 to 6
- storage: float32 [256, 2048], P('gy', 'gx'), may hold values from 0.5 to 4
- leakage: float32 [256, 2048], P('gy', 'gx'), may hold values from 0.1 to 1
- cond_east: float32 [256, 2048], P('gy', 'gx'), may hold values from 0.5 to 2
- cond_south: float32 [256, 2048], P('gy', 'gx'), may hold values from 0.5 to 2
- owner_weight: int32 [256, 2048], P('gy', 'gx'), may hold values from 1 to 3
- aggregate: int32 [256, 2048], P('gy', 'gx'), may hold values from 0 to 2047, as said below
- coarse_inverse: float32 [2048, 2048], P(('gx', 'gy')), as said below
Outputs:
- relaxed: float32 [32, 256, 2048], P(None, 'gy', 'gx')
Inputs may be any that keep to these rules, and one draw needn't show every extreme that they name: coarse_inverse is exactly symmetric, with diagonal entries from 1 / 256 to 4 / 256. `aggregate`: the nodes of tile (a, b) carry exactly the aggregates (b * 4 + a) * 64 to (b * 4 + a + 1) * 64 - 1, each of them inside that tile.
All inputs are finite; a program needn't handle non-finite values.
Results may differ from a plain program's by a relative error of at most 0.0003.
Values sent between devices are 32-bit elements; how exact they have to be, the bound alone decides.
A program may use at most 128 MiB of HBM per device.

v0:
```python
import functools

import jax
import jax.numpy as jnp
from jax import lax
from jax.experimental import pallas as pl
from jax.experimental.pallas import tpu as pltpu
from jax.sharding import PartitionSpec as P

DEG = 8
OV = 2
HALO = OV + 1
LANES = 128
VR = 9
ROWS_L = 8 * VR
COEFS = 6
DELTA = 0.95
SIGMA = 1.0 / DELTA
OFFSETS = (0, 67, 134)
SPLIT_AB, SPLIT_BC = 98, 164
F32 = jnp.float32
BF16 = jnp.bfloat16
MESH = pl.DeviceIdType.MESH
VMEM_LIMIT = 56 * 1024 * 1024


def lane_id():
    return lax.broadcasted_iota(jnp.int32, (8, LANES), 1)


def sub_id():
    return lax.broadcasted_iota(jnp.int32, (8, LANES), 0)


def turn(x, by):
    by = by % LANES
    return pltpu.roll(x, by, 1) if not (isinstance(by, int) and by == 0) else x


def position(axes):
    gx, gy = lax.axis_index("gx"), lax.axis_index("gy")
    return gx > 0, gx < axes[0] - 1, gy > 0, gy < axes[1] - 1


def masked_coefs(refs, rows, half, axes, first_row):
    _, has_e, _, has_s = position(axes)
    start, sto, leak, east, south, owner = [ref[rows, :] for ref in refs]
    if half == 1:
        cut = jnp.logical_and(lane_id() == LANES - 1, jnp.logical_not(has_e))
        east = jnp.where(cut, 0.0, east)
    cut = jnp.logical_and(sub_id() + first_row == 63, jnp.logical_not(has_s))
    south = jnp.where(cut, 0.0, south)
    return start, sto, leak, east, south, owner.astype(F32)


def pack_kernel(axes, steps, rows, *refs):
    prev, src = refs[0:2], refs[2:4]
    coef = [refs[4 + 2 * p : 6 + 2 * p] for p in range(COEFS)]
    xw, xe, yn, ys = refs[4 + 2 * COEFS :]
    group = lane_id() // 4

    @pl.loop(0, rows // 8)
    def _(t):
        first = pl.multiple_of(t * 8, 8)
        for k, arr in enumerate((prev, src)):
            low = jnp.zeros((8, LANES), F32)
            high = jnp.zeros((8, LANES), F32)
            for n in range(steps):
                at = pl.ds(pl.multiple_of(n * rows + first, 8), 8)
                low = jnp.where(group == n, turn(arr[0][at, :], 4 * n), low)
                high = jnp.where(group == n, turn(arr[1][at, :], 4 * n - 125), high)
            xw[k, pl.ds(first, 8), :] = low
            xe[k, pl.ds(first, 8), :] = high
        at = pl.ds(first, 8)
        low = jnp.zeros((8, LANES), F32)
        high = jnp.zeros((8, LANES), F32)
        planes0 = masked_coefs([c[0] for c in coef], at, 0, axes, first)
        planes1 = masked_coefs([c[1] for c in coef], at, 1, axes, first)
        for p in range(COEFS):
            low = jnp.where(group == p, turn(planes0[p], 4 * p), low)
            high = jnp.where(group == p, turn(planes1[p], 4 * p - 125), high)
        xw[2, at, :] = low
        xe[2, at, :] = high

    for out, first, base in ((yn, 0, 0), (ys, rows - HALO, rows - 8)):
        for h in range(2):
            for j in range(HALO):
                for k, arr in enumerate((prev, src)):
                    for q in range(steps // 8):
                        start = 8 * q * rows + first + j
                        out[h, j, k * steps + 8 * q : k * steps + 8 * q + 8, :] = arr[h][
                            pl.ds(start, 8, stride=rows), :
                        ]
            planes = masked_coefs([c[h] for c in coef], pl.ds(base, 8), h, axes, base)
            for j in range(HALO):
                at = first + j - base
                pieces = [p[at : at + 1] for p in planes]
                pieces += [jnp.zeros((8 - COEFS, LANES), F32)]
                out[h, j, 2 * steps : 2 * steps + 8, :] = jnp.concatenate(pieces, 0)


def exchange_kernel(axes, xw, xe, yn, ys, *refs):
    outs = refs[:8]
    send, recv = refs[8:]
    n_x, n_y = axes
    gx, gy = lax.axis_index("gx"), lax.axis_index("gy")
    west, east = lax.rem(gx + n_x - 1, n_x), lax.rem(gx + 1, n_x)
    north, south = lax.rem(gy + n_y - 1, n_y), lax.rem(gy + 1, n_y)
    from_w, from_e, from_n, from_s, from_nw, from_ne, from_sw, from_se = outs
    last = yn.shape[0] - 1
    plan = (
        (yn, from_s, (gx, north)),
        (ys, from_n, (gx, south)),
        (xw, from_e, (west, gy)),
        (xe, from_w, (east, gy)),
        (yn.at[0], from_se, (west, north)),
        (yn.at[last], from_sw, (east, north)),
        (ys.at[0], from_ne, (west, south)),
        (ys.at[last], from_nw, (east, south)),
    )
    barrier = pltpu.get_barrier_semaphore()
    for _, _, to in plan:
        pl.semaphore_signal(barrier, inc=1, device_id=to, device_id_type=MESH)
    pl.semaphore_wait(barrier, len(plan))
    copies = []
    for i, (src, dst, to) in enumerate(plan):
        copy = pltpu.make_async_remote_copy(
            src_ref=src, dst_ref=dst, send_sem=send.at[i], recv_sem=recv.at[i],
            device_id=to, device_id_type=MESH,
        )
        copy.start()
        copies.append(copy)
    for copy in copies:
        copy.wait()


def exchange(axes, ident, xw, xe, yn, ys):
    corner = jax.ShapeDtypeStruct(yn.shape[1:], F32)
    shape = lambda a: jax.ShapeDtypeStruct(a.shape, F32)
    return pl.pallas_call(
        functools.partial(exchange_kernel, axes),
        out_shape=[shape(xw), shape(xw), shape(yn), shape(yn)] + [corner] * 4,
        in_specs=[pl.BlockSpec(memory_space=pl.ANY)] * 4,
        out_specs=[pl.BlockSpec(memory_space=pl.ANY)] * 8,
        scratch_shapes=[pltpu.SemaphoreType.DMA((8,)), pltpu.SemaphoreType.DMA((8,))],
        compiler_params=pltpu.CompilerParams(collective_id=ident, has_side_effects=True),
        name="neighbour_exchange",
    )(xw, xe, yn, ys)


def lay(a, b, west, east):
    lane = lane_id()
    first = jnp.where(lane < HALO, west, turn(a, HALO))
    mid = jnp.where(lane < 64, turn(a, 64), turn(b, 64))
    last = jnp.where(lane >= LANES - HALO, turn(east, LANES - HALO), turn(b, LANES - HALO))
    return first, mid, last


def sweep_kernel(axes, steps, rows, *refs):
    prev, src = refs[0:2], refs[2:4]
    coef = [refs[4 + 2 * p : 6 + 2 * p] for p in range(COEFS)]
    base = 4 + 2 * COEFS
    from_w, from_e, from_n, from_s, from_nw, from_ne, from_sw, from_se = refs[base : base + 8]
    waves, co, xw, xe, yn, ys = refs[base + 8 : base + 14]
    ext, cc, gbuf, carry = refs[base + 14 :]
    has_w, has_e, has_n, has_s = position(axes)
    lane, sub = lane_id(), sub_id()
    zero = jnp.zeros((8, LANES), F32)

    def keep(flag, value):
        return jnp.where(flag, value, 0.0)

    def put_own(plane, t, a, b, k, slot):
        at = pl.ds(t * 8, 8)
        west = keep(has_w, turn(from_w[k, at, :], -4 * slot + LANES * 4))
        east = keep(has_e, turn(from_e[k, at, :], -4 * slot + LANES * 4))
        for g, value in enumerate(lay(a, b, west, east)):
            ext[g, pl.ds(plane * ROWS_L + HALO + 8 * t, 8), :] = value

    @pl.loop(0, steps)
    def _(n):
        for k, arr in enumerate((prev, src)):
            for t in range(rows // 8):
                at = pl.ds(pl.multiple_of(n * rows + 8 * t, 8), 8)
                put_own(k * steps + n, t, arr[0][at, :], arr[1][at, :], k, n)

    for t in range(rows // 8):
        at = pl.ds(8 * t, 8)
        planes0 = masked_coefs([c[0] for c in coef], at, 0, axes, 8 * t)
        planes1 = masked_coefs([c[1] for c in coef], at, 1, axes, 8 * t)
        for p in range(COEFS):
            put_own(2 * steps + p, t, planes0[p], planes1[p], 2, p)
    for j in range(HALO):
        for strip, cw, ce, flag, row in (
            (from_n, from_nw, from_ne, has_n, j),
            (from_s, from_sw, from_se, has_s, rows + HALO + j),
        ):
            for q in range(2 * steps // 8 + 1):
                at = pl.ds(8 * q, 8)
                a = keep(flag, strip[0, j, at, :])
                b = keep(flag, strip[1, j, at, :])
                west = keep(jnp.logical_and(flag, has_w), turn(cw[j, at, :], -125))
                east = keep(jnp.logical_and(flag, has_e), ce[j, at, :])
                for g, value in enumerate(lay(a, b, west, east)):
                    ext[g, pl.ds(8 * q * ROWS_L + row, 8, stride=ROWS_L), :] = value
    for row in range(rows + 2 * HALO, ROWS_L):
        for q in range(2 * steps // 8 + 1):
            for g in range(3):
                ext[g, pl.ds(8 * q * ROWS_L + row, 8, stride=ROWS_L), :] = zero

    def plane(index, v, g):
        return ext[g, pl.ds(index * ROWS_L + v, 8, stride=VR), :]

    first_coef = 2 * steps
    for g in range(3):
        col = lane + OFFSETS[g]
        col_in = jnp.logical_and(col >= 1, col <= 260)
        col_own = jnp.logical_and(col >= HALO, col <= 258)
        col_there = jnp.logical_and(
            jnp.logical_or(col >= HALO, has_w), jnp.logical_or(col <= 258, has_e)
        )
        n_cols = (
            1.0
            + jnp.where(jnp.logical_and(col <= 4, has_w), 1.0, 0.0)
            + jnp.where(jnp.logical_and(col >= 257, has_e), 1.0, 0.0)
        )
        souths = [plane(first_coef + 4, v, g) for v in range(VR)]
        for v in range(VR):
            row = sub * VR + v
            row_in = jnp.logical_and(row >= 1, row <= 68)
            row_own = jnp.logical_and(row >= HALO, row <= 66)
            row_there = jnp.logical_and(
                jnp.logical_or(row >= HALO, has_n), jnp.logical_or(row <= 66, has_s)
            )
            inner = jnp.logical_and(row_in, col_in)
            own = jnp.logical_and(row_own, col_own)
            there = jnp.logical_and(jnp.logical_and(row_there, col_there), inner)
            n_rows = (
                1.0
                + jnp.where(jnp.logical_and(row <= 4, has_n), 1.0, 0.0)
                + jnp.where(jnp.logical_and(row >= 65, has_s), 1.0, 0.0)
            )
            start, sto, leak, east, south, owner = [
                plane(first_coef + p, v, g) for p in range(COEFS)
            ]
            ea_w = turn(east, 1)
            so_n = souths[v - 1] if v else pltpu.roll(souths[VR - 1], 1, 0)
            diag = sto + leak + east + ea_w + south + so_n
            safe = jnp.where(there, diag, 1.0)
            scale = jnp.where(there, 2.0 * SIGMA / safe, 0.0)
            cc[0, g, v] = jnp.where(lane == LANES - 1, 0.0, scale * east)
            cc[1, g, v] = jnp.where(lane == 0, 0.0, scale * ea_w)
            cc[2, g, v] = scale * south
            cc[3, g, v] = scale * so_n
            cc[4, g, v] = scale
            cc[5, g, v] = scale * sto
            cc[6, g, v] = jnp.where(inner, 0.0, 2.0 * SIGMA)
            weight = jnp.where(own, owner, jnp.where(there, 1.0, 0.0))
            cc[7, g, v] = weight * (1.0 / TAU[DEG])
            den = jnp.where(there, owner + n_rows * n_cols - 1.0, 1.0)
            at = slice(8 * v, 8 * v + 8)
            co[0, g, at, :] = weight
            co[1, g, at, :] = jnp.where(there, 1.0 / den, 0.0)
            co[2, g, at, :] = diag
            co[3, g, at, :] = east
            co[4, g, at, :] = ea_w
            co[5, g, at, :] = south
            co[6, g, at, :] = so_n
            co[7, g, at, :] = sto
            co[8, g, at, :] = start
            carry[g, v] = start

    xw[...] = jnp.zeros_like(xw)
    xe[...] = jnp.zeros_like(xe)
    group = lane // 4

    def stencil(y, g, v):
        cur = y[g][v]
        down = y[g][v + 1] if v < VR - 1 else pltpu.roll(y[g][0], 7, 0)
        up = y[g][v - 1] if v else pltpu.roll(y[g][VR - 1], 1, 0)
        return (
            cc[0, g, v] * turn(cur, LANES - 1)
            + cc[1, g, v] * turn(cur, 1)
            + (cc[2, g, v] * down + cc[3, g, v] * up)
        )

    def advance(n, held):
        old = [[None] * VR for _ in range(3)]
        for g in range(3):
            for v in range(VR):
                old[g][v] = plane(n, v, g)
                gbuf[g, v] = (
                    cc[4, g, v] * plane(steps + n, v, g)
                    + cc[5, g, v] * held[g][v]
                    + cc[6, g, v] * old[g][v]
                )
        now = [
            [0.5 * (stencil(old, g, v) + gbuf[g, v]) for v in range(VR)] for g in range(3)
        ]
        for k in range(1, DEG):
            new = [
                [stencil(now, g, v) + (TAU[k] * gbuf[g, v] - old[g][v]) for v in range(VR)]
                for g in range(3)
            ]
            old, now = now, new
        return now

    def finish(n, now):
        for g in range(3):
            for v in range(VR):
                at = pl.ds(pl.multiple_of(n * ROWS_L + 8 * v, 8), 8)
                waves[g, at, :] = now[g][v] * (1.0 / TAU[DEG])
        weighted = [[cc[7, g, v] * now[g][v] for v in range(VR)] for g in range(3)]
        for v in range(VR):
            at = slice(8 * v, 8 * v + 8)
            xw[at, :] = jnp.where(group == n, turn(weighted[0][v], 4 * n + LANES - 1), xw[at, :])
            xe[at, :] = jnp.where(group == n, turn(weighted[2][v], 4 * n + 4), xe[at, :])
        for j in range(HALO):
            for g in range(3):
                yn[g, j, pl.ds(n, 1), :] = weighted[g][1 + j][0:1]
                ys[g, j, pl.ds(n, 1), :] = weighted[g][3 + j][7:8]
        return [[now[g][v] * (1.0 / TAU[DEG]) for v in range(VR)] for g in range(3)]

    @pl.loop(0, steps)
    def _(n):
        held = [[carry[g, v] for v in range(VR)] for g in range(3)]
        held = finish(n, advance(n, held))
        for v in range(VR):
            a, b, c = held[0][v], held[1][v], held[2][v]
            carry[0, v] = jnp.where(lane < SPLIT_AB, a, turn(b, 67))
            left = jnp.where(lane < SPLIT_AB - 67, turn(a, 61), b)
            carry[1, v] = jnp.where(lane < SPLIT_BC - 67, left, turn(c, 67))
            carry[2, v] = jnp.where(lane < SPLIT_BC - 134, turn(b, 61), c)


def chebyshev_scales():
    tau = [1.0, SIGMA]
    for _ in range(DEG):
        tau.append(2.0 * SIGMA * tau[-1] - tau[-2])
    return tau


TAU = chebyshev_scales()


def one_hot_of(row, count, first):
    ids = jnp.broadcast_to(row - first, (count, row.shape[1]))
    return jnp.where(
        ids == lax.broadcasted_iota(jnp.int32, ids.shape, 0), 1.0, 0.0
    ).astype(BF16)


def settle_kernel(axes, steps, rows, aggs, *refs):
    waves, co, from_w, from_e, from_n, from_s, from_nw, from_ne, from_sw, from_se = refs[:10]
    src = refs[10:12]
    agg = refs[12]
    settled, coarse = refs[13:15]
    before, rest = refs[15:]
    has_w, has_e, has_n, has_s = position(axes)
    lane, sub = lane_id(), sub_id()
    tile = lax.axis_index("gx") * axes[1] + lax.axis_index("gy")

    for g in range(3):
        for v in range(VR):
            before[g, v] = co[8, g, 8 * v : 8 * v + 8, :]

    west_lanes = jnp.logical_and(jnp.logical_and(lane >= 2, lane <= 4), has_w)
    east_lanes = jnp.logical_and(jnp.logical_and(lane >= 123, lane <= 125), has_e)
    top, bottom = jnp.logical_and(sub == 0, has_n), jnp.logical_and(sub == 7, has_s)

    def spread(row):
        return jnp.broadcast_to(row, (8, LANES))

    @pl.loop(0, steps)
    def _(n):
        now = [[None] * VR for _ in range(3)]
        for v in range(VR):
            at = slice(8 * v, 8 * v + 8)
            for g in range(3):
                here = pl.ds(pl.multiple_of(n * ROWS_L + 8 * v, 8), 8)
                total = co[0, g, at, :] * waves[g, here, :]
                if g == 0:
                    total += jnp.where(west_lanes, turn(from_w[at, :], 2 - 4 * n + 4 * LANES), 0.0)
                if g == 2:
                    total += jnp.where(east_lanes, turn(from_e[at, :], 123 - 4 * n + 4 * LANES), 0.0)
                if 2 <= v <= 4:
                    one = pl.ds(n, 1)
                    total += jnp.where(top, spread(from_n[g, v - 2, one, :]), 0.0)
                    total += jnp.where(bottom, spread(from_s[g, v - 2, one, :]), 0.0)
                    if g == 0:
                        for flag, ref in ((top, from_nw), (bottom, from_sw)):
                            piece = turn(spread(ref[v - 2, one, :]), 2 - 124)
                            total += jnp.where(jnp.logical_and(flag, west_lanes), piece, 0.0)
                    if g == 2:
                        for flag, ref in ((top, from_ne), (bottom, from_se)):
                            piece = turn(spread(ref[v - 2, one, :]), 123 - 1)
                            total += jnp.where(jnp.logical_and(flag, east_lanes), piece, 0.0)
                now[g][v] = total * co[1, g, at, :]
        out = [[None] * VR for _ in range(3)]
        for g in range(3):
            for v in range(VR):
                at = slice(8 * v, 8 * v + 8)
                cur = now[g][v]
                down = now[g][v + 1] if v < VR - 1 else pltpu.roll(now[g][0], 7, 0)
                up = now[g][v - 1] if v else pltpu.roll(now[g][VR - 1], 1, 0)
                image = (
                    co[2, g, at, :] * cur
                    - co[3, g, at, :] * turn(cur, LANES - 1)
                    - co[4, g, at, :] * turn(cur, 1)
                    - co[5, g, at, :] * down
                    - co[6, g, at, :] * up
                )
                out[g][v] = co[7, g, at, :] * before[g, v] - image
                before[g, v] = cur
        for v in range(VR):
            at = pl.ds(n * ROWS_L + v, 8, stride=VR)
            for ref, values in ((settled, now), (rest, out)):
                a, b, c = values[0][v], values[1][v], values[2][v]
                mid = turn(b, 64)
                ref[0, at, :] = jnp.where(lane < SPLIT_AB - HALO, turn(a, -HALO), mid)
                ref[1, at, :] = jnp.where(lane < SPLIT_BC - 131, mid, turn(c, HALO))

    def add_row(row, total):
        rest_at = pl.ds(row + HALO, steps, stride=ROWS_L)
        src_at = pl.ds(row, steps, stride=rows)
        values = jnp.concatenate([rest[h, rest_at, :] + src[h][src_at, :] for h in range(2)], 1)
        high = values.astype(BF16)
        low = (values - high.astype(F32)).astype(BF16)
        hot = one_hot_of(agg[pl.ds(row, 1), :], aggs, tile * aggs)
        return total + lax.dot_general(
            jnp.concatenate([high, low], 0), hot, (((1,), (1,)), ((), ())),
            preferred_element_type=F32,
        )

    def add_rows(i, total):
        for k in range(4):
            total = add_row(4 * i + k, total)
        return total

    total = lax.fori_loop(0, rows // 4, add_rows, jnp.zeros((2 * steps, aggs), F32))
    total = total[:steps] + total[steps:]
    coarse[...] = jnp.concatenate([total[: steps // 2], total[steps // 2 :]], 1)


def gather_kernel(axes, own, everyone, send, recv, local):
    n_x, n_y = axes
    count = n_x * n_y
    me = lax.axis_index("gx") * n_y + lax.axis_index("gy")

    def other(i):
        which = lax.rem(me + i, count)
        return which // n_y, lax.rem(which, n_y)

    barrier = pltpu.get_barrier_semaphore()

    @pl.loop(1, count)
    def _(i):
        pl.semaphore_signal(barrier, inc=1, device_id=other(i), device_id_type=MESH)

    pl.semaphore_wait(barrier, count - 1)
    mine = pltpu.make_async_copy(own, everyone.at[me], local)
    mine.start()

    def copy(i):
        return pltpu.make_async_remote_copy(
            src_ref=own, dst_ref=everyone.at[me], send_sem=send.at[i], recv_sem=recv.at[i],
            device_id=other(i), device_id_type=MESH,
        )

    @pl.loop(1, count)
    def _(i):
        copy(i).start()

    @pl.loop(1, count)
    def _(i):
        source = lax.rem(me + count - i, count)
        pltpu.make_async_remote_copy(
            src_ref=own, dst_ref=everyone.at[source], send_sem=send.at[i], recv_sem=recv.at[i],
            device_id=other(i), device_id_type=MESH,
        ).wait()

    mine.wait()


def gather(axes, ident, own):
    count = axes[0] * axes[1]
    return pl.pallas_call(
        functools.partial(gather_kernel, axes),
        out_shape=jax.ShapeDtypeStruct((count,) + own.shape, F32),
        in_specs=[pl.BlockSpec(memory_space=pl.ANY)],
        out_specs=pl.BlockSpec(memory_space=pl.ANY),
        scratch_shapes=[
            pltpu.SemaphoreType.DMA((count,)),
            pltpu.SemaphoreType.DMA((count,)),
            pltpu.SemaphoreType.DMA,
        ],
        compiler_params=pltpu.CompilerParams(collective_id=ident, has_side_effects=True),
        name="coarse_gather",
    )(own)


def correct_kernel(axes, steps, rows, aggs, everyone, inverse, agg, settled, out, fixed):
    tile = lax.axis_index("gx") * axes[1] + lax.axis_index("gy")
    count = axes[0] * axes[1]

    @pl.when(pl.program_id(0) == 0)
    def _():
        low_lanes = lax.broadcasted_iota(jnp.int32, (steps // 2, LANES), 1) < aggs
        total = jnp.zeros((steps, aggs), F32)
        for d in range(0, count, 2):
            a, b = everyone[d], everyone[d + 1]
            upper = jnp.where(low_lanes, a, pltpu.roll(b, aggs, 1))
            lower = jnp.where(low_lanes, pltpu.roll(a, aggs, 1), b)
            total += lax.dot_general(
                jnp.concatenate([upper, lower], 0),
                inverse[:, d * aggs : (d + 2) * aggs],
                (((1,), (1,)), ((), ())),
                precision=lax.Precision.HIGHEST,
                preferred_element_type=F32,
            )
        high = total.astype(BF16)
        low = (total - high.astype(F32)).astype(BF16)
        fixed[...] = jnp.concatenate([high, low], 1)

    factor = fixed[...]

    @pl.loop(0, rows // 4)
    def _(i):
        for k in range(4):
            row = 4 * i + k
            hot = one_hot_of(agg[pl.ds(row, 1), :], aggs, tile * aggs)
            grown = jnp.dot(
                factor, jnp.concatenate([hot, hot], 0), preferred_element_type=F32
            )
            out[pl.ds(row, steps, stride=rows), :] = (
                settled[0, pl.ds(row + HALO, steps, stride=ROWS_L), :] + grown
            )


def halves(shape):
    block = (shape[0], LANES)
    return [pl.BlockSpec(block, lambda i: (0, 0)), pl.BlockSpec(block, lambda i: (0, 1))]


def whole(shape):
    return pl.BlockSpec(shape, lambda i: (0,) * len(shape))


def shards(axes, prev_wave, source, start_state, storage, leakage, cond_east, cond_south,
           owner_weight, aggregate, coarse_inverse):
    steps, rows, cols = prev_wave.shape
    aggs = coarse_inverse.shape[0]
    planes = 2 * steps + 8
    flat = (steps * rows, cols)
    prev, src = prev_wave.reshape(flat), source.reshape(flat)
    coef = (start_state, storage, leakage, cond_east, cond_south, owner_weight)
    params = pltpu.CompilerParams(vmem_limit_bytes=VMEM_LIMIT)
    fields, field_specs = [], []
    for arr in (prev, src) + coef:
        fields += [arr, arr]
        field_specs += halves(arr.shape)

    def local(kernel, name, args, in_specs, outs, scratch):
        return pl.pallas_call(
            kernel,
            grid=(1,),
            out_shape=[jax.ShapeDtypeStruct(s, F32) for s in outs],
            in_specs=in_specs,
            out_specs=[whole(s) for s in outs],
            scratch_shapes=scratch,
            compiler_params=params,
            name=name,
        )(*args)

    strips = local(
        functools.partial(pack_kernel, axes, steps, rows), "halo_pack", fields, field_specs,
        [(3, rows, LANES)] * 2 + [(cols // LANES, HALO, planes, LANES)] * 2, [],
    )
    halo = exchange(axes, 0, *strips)
    waves, co, *rims = local(
        functools.partial(sweep_kernel, axes, steps, rows), "local_sweep",
        fields + list(halo), field_specs + [whole(h.shape) for h in halo],
        [(3, steps * ROWS_L, LANES), (9, 3, ROWS_L, LANES)]
        + [(ROWS_L, LANES)] * 2 + [(3, HALO, steps, LANES)] * 2,
        [
            pltpu.VMEM((3, planes * ROWS_L, LANES), F32),
            pltpu.VMEM((8, 3, VR, 8, LANES), F32),
            pltpu.VMEM((3, VR, 8, LANES), F32),
            pltpu.VMEM((3, VR, 8, LANES), F32),
        ],
    )
    rim = exchange(axes, 1, *rims)
    args = [waves, co, *rim]
    settled, coarse = local(
        functools.partial(settle_kernel, axes, steps, rows, aggs), "settle_and_restrict",
        args + [src, src, aggregate],
        [whole(a.shape) for a in args] + halves(flat) + [whole(aggregate.shape)],
        [(2, steps * ROWS_L, LANES), (steps // 2, 2 * aggs)],
        [pltpu.VMEM((3, VR, 8, LANES), F32), pltpu.VMEM((2, steps * ROWS_L, LANES), F32)],
    )
    everyone = gather(axes, 2, coarse)
    out = pl.pallas_call(
        functools.partial(correct_kernel, axes, steps, rows, aggs),
        grid=(2,),
        out_shape=jax.ShapeDtypeStruct(flat, F32),
        in_specs=[
            whole(everyone.shape),
            whole(coarse_inverse.shape),
            pl.BlockSpec((rows, LANES), lambda i: (0, i)),
            pl.BlockSpec((1, steps * ROWS_L, LANES), lambda i: (i, 0, 0)),
        ],
        out_specs=pl.BlockSpec((steps * rows, LANES), lambda i: (0, i)),
        scratch_shapes=[pltpu.VMEM((steps, 2 * aggs), BF16)],
        compiler_params=params,
        name="correct",
    )(everyone, coarse_inverse, aggregate, settled)
    return out.reshape(prev_wave.shape)


def solution(mesh):
    axes = (mesh.shape["gx"], mesh.shape["gy"])
    plane = P("gy", "gx")
    wave = P(None, "gy", "gx")
    return jax.shard_map(
        functools.partial(shards, axes),
        mesh=mesh,
        in_specs=(wave, wave) + (plane,) * 7 + (P(("gx", "gy"), None),),
        out_specs=wave,
        check_vma=False,
    )
```

profile of v0, /device:TPU:1, one launch (start us, length us, event | category | flops | bytes accessed | tf_op | source)
XLA Modules:
  0.0 121.4 jit_solution(10576318577695330016)
XLA Ops:
  0.0 4.9 %halo_pack.1 = (f32[3,64,128]{2,1,0:T(8,128)}, f32[3,64,128]{2,1,0:T(8,128)}, f32[2,3,72,128]{3,2,1,0:T(8,128)}, f32[2,3,72,128]{3,2,1,0:T(8,128)}) custom-call(f32[2048,256]{1,0:T(8,128)} %bitcast.9, f32[2048,256]{1,0:T(8,128)} %bitcast.10, f32[2048,256]{1,0:T(8,128)} %bitcast.3, f32[2048,256]{1,0:T(8,128)} %bitcast.4, f32[64,256]{1,0:T(8,128)} %refs_5_.3, ...), custom_call_target="tpu_custom_call" | custom-call | tf_op jit(solution)/shard_map/halo_pack/pallas_call | solution.py:564
  4.9 25.2 %neighbour_exchange.2 = (f32[3,64,128]{2,1,0:T(8,128)}, f32[3,64,128]{2,1,0:T(8,128)}, f32[2,3,72,128]{3,2,1,0:T(8,128)}, f32[2,3,72,128]{3,2,1,0:T(8,128)}, f32...) custom-call(f32[3,64,128]{2,1,0:T(8,128)} %get-tuple-element.33.xw, ...), custom_call_target="tpu_custom_call" | custom-call | tf_op jit(solution)/shard_map/neighbour_exchange/pallas_call | solution.py:140
  30.2 38.1 %local_sweep.1 = (f32[3,2304,128]{2,1,0:T(8,128)}, f32[9,3,72,128]{3,2,1,0:T(8,128)}, f32[72,128]{1,0:T(8,128)}, f32[72,128]{1,0:T(8,128)}, f32[3,3,32,128]{3,2,1,0:T(8,128)}, /*index=5*/f32[3,3,32,128]{3,2,1,0:T(8,128)}) custom-call(f32[2048,256]{1,0:T(8,128)} %bitcast.11, f32[2048,256]{1,0:T(8,128)} %bitcast.12, f32[2048,256]{1,0:T(8,128)} %bitcast.5, ...), custom_call_target="tpu_custom_call" | custom-call | tf_op jit(solution)/shard_map/local_sweep/pallas_call | solution.py:564
  68.3 15.5 %neighbour_exchange.3 = (f32[72,128]{1,0:T(8,128)}, f32[72,128]{1,0:T(8,128)}, f32[3,3,32,128]{3,2,1,0:T(8,128)}, f32[3,3,32,128]{3,2,1,0:T(8,128)}, f32[3,32,12...) custom-call(f32[72,128]{1,0:T(8,128)} %get-tuple-element.47.xw, ...), custom_call_target="tpu_custom_call" | custom-call | tf_op jit(solution)/shard_map/neighbour_exchange/pallas_call | solution.py:140
  83.8 17.1 %settle_and_restrict.1 = (f32[2,2304,128]{2,1,0:T(8,128)}, f32[16,128]{1,0:T(8,128)}) custom-call(f32[3,2304,128]{2,1,0:T(8,128)} %get-tuple-element.45.refs_0_, f32[9,3,72,128]{3,2,1,0:T(8,128)} %get-tuple-element.46.refs_1_, f32[72,128]{1,0:T(8,128)} %get-tuple-element.51.refs_2_, f32[72,128]{1,0:T(8,128)} %get-tuple-element.52.refs_3_, ...), custom_call_target="tpu_custom_call" | custom-call | tf_op jit(solution)/shard_map/settle_and_restrict/pallas_call | solution.py:564
  100.9 11.1 %coarse_gather.1.everyone = f32[32,16,128]{2,1,0:T(8,128)} custom-call(f32[16,128]{1,0:T(8,128)} %get-tuple-element.59.own), custom_call_target="tpu_custom_call" | custom-call | tf_op jit(solution)/shard_map/coarse_gather/pallas_call | solution.py:487
  112.0 9.4 %correct.1 = f32[2048,256]{1,0:T(8,128)} custom-call(f32[32,16,128]{2,1,0:T(8,128)} %coarse_gather.1.everyone, f32[64,2048]{1,0:T(8,128)} %inverse.1, s32[64,256]{1,0:T(8,128)} %agg.1, f32[2,2304,128]{2,1,0:T(8,128)} %get-tuple-element.60.settled), custom_call_target="tpu_custom_call" | custom-call | tf_op jit(solution)/shard_map/correct/pallas_call | solution.py:602
where the time goes:
time: 122 us; the launch traced here: 121 us
  Pallas kernels  121 us (99%)
    pallas_call x3, Pallas kernels, local(): pl.pallas_call(kernel, grid=(1,), out_shape=[jax.ShapeDtypeStruct(s, F32)...  60.2 us
    pallas_call x2, Pallas kernels, exchange(): pl.pallas_call(functools.partial(exchange_kernel, axes), out_shape=[shape...  40.7 us
    pallas_call x1, Pallas kernels, gather(): pl.pallas_call(functools.partial(gather_kernel, axes), out_shape=jax.Shap...  11.1 us
    pallas_call x1, Pallas kernels, shards(): pl.pallas_call(functools.partial(correct_kernel, axes, steps, rows, aggs)...  9.39 us

commit v1 on v0

--- a/solution.py
+++ b/solution.py
@@ -56,7 +56,7 @@
 def pack_kernel(axes, steps, rows, *refs):
     prev, src = refs[0:2], refs[2:4]
     coef = [refs[4 + 2 * p : 6 + 2 * p] for p in range(COEFS)]
-    xw, xe, yn, ys = refs[4 + 2 * COEFS :]
+    xw, xe, yn, ys, *corners = refs[4 + 2 * COEFS :]
     group = lane_id() // 4
 
     @pl.loop(0, rows // 8)
@@ -82,70 +82,86 @@
         xw[2, at, :] = low
         xe[2, at, :] = high
 
-    for out, first, base in ((yn, 0, 0), (ys, rows - HALO, rows - 8)):
+    for side, (out, first, base) in enumerate(((yn, 0, 0), (ys, rows - HALO, rows - 8))):
         for h in range(2):
-            for j in range(HALO):
-                for k, arr in enumerate((prev, src)):
-                    for q in range(steps // 8):
-                        start = 8 * q * rows + first + j
-                        out[h, j, k * steps + 8 * q : k * steps + 8 * q + 8, :] = arr[h][
-                            pl.ds(start, 8, stride=rows), :
-                        ]
             planes = masked_coefs([c[h] for c in coef], pl.ds(base, 8), h, axes, base)
-            for j in range(HALO):
-                at = first + j - base
-                pieces = [p[at : at + 1] for p in planes]
-                pieces += [jnp.zeros((8 - COEFS, LANES), F32)]
-                out[h, j, 2 * steps : 2 * steps + 8, :] = jnp.concatenate(pieces, 0)
-
-
-def exchange_kernel(axes, xw, xe, yn, ys, *refs):
+            corner = jnp.zeros((8, LANES), F32)
+            for q, j, at in strip_blocks(steps, side):
+                if q < 2 * steps // 8:
+                    arr, part = (prev, q) if q < steps // 8 else (src, q - steps // 8)
+                    value = arr[h][pl.ds(8 * part * rows + first + j, 8, stride=rows), :]
+                else:
+                    row = first + j - base
+                    pieces = [p[row : row + 1] for p in planes]
+                    value = jnp.concatenate(pieces + [jnp.zeros((8 - COEFS, LANES), F32)], 0)
+                out[h, at : at + 8, :] = value
+                slot = 4 * (HALO * q + j)
+                corner = jnp.where(group == slot // 4, turn(value, slot - (0, 125)[h]), corner)
+            corners[2 * side + h][...] = corner
+
+
+def strip_blocks(steps, side):
+    at, blocks = 0, []
+    for q in range(2 * steps // 8 + 1):
+        for j in range(HALO):
+            if steps // 8 <= q < 2 * steps // 8 and j == (HALO - 1, 0)[side]:
+                continue
+            blocks.append((q, j, at))
+            at += 8
+    return blocks
+
+
+def exchange_kernel(axes, xw, xe, yn, ys, c_nw, c_ne, c_sw, c_se, *refs):
     outs = refs[:8]
     send, recv = refs[8:]
-    n_x, n_y = axes
     gx, gy = lax.axis_index("gx"), lax.axis_index("gy")
-    west, east = lax.rem(gx + n_x - 1, n_x), lax.rem(gx + 1, n_x)
-    north, south = lax.rem(gy + n_y - 1, n_y), lax.rem(gy + 1, n_y)
+    has_w, has_e, has_n, has_s = position(axes)
+    west, east, north, south = gx - 1, gx + 1, gy - 1, gy + 1
+    both = jnp.logical_and
+    has_nw, has_ne = both(has_n, has_w), both(has_n, has_e)
+    has_sw, has_se = both(has_s, has_w), both(has_s, has_e)
     from_w, from_e, from_n, from_s, from_nw, from_ne, from_sw, from_se = outs
-    last = yn.shape[0] - 1
     plan = (
-        (yn, from_s, (gx, north)),
-        (ys, from_n, (gx, south)),
-        (xw, from_e, (west, gy)),
-        (xe, from_w, (east, gy)),
-        (yn.at[0], from_se, (west, north)),
-        (yn.at[last], from_sw, (east, north)),
-        (ys.at[0], from_ne, (west, south)),
-        (ys.at[last], from_nw, (east, south)),
+        (yn, from_s, (gx, north), has_n, has_s),
+        (ys, from_n, (gx, south), has_s, has_n),
+        (xw, from_e, (west, gy), has_w, has_e),
+        (xe, from_w, (east, gy), has_e, has_w),
+        (c_nw, from_se, (west, north), has_nw, has_se),
+        (c_ne, from_sw, (east, north), has_ne, has_sw),
+        (c_sw, from_ne, (west, south), has_sw, has_ne),
+        (c_se, from_nw, (east, south), has_se, has_nw),
     )
     barrier = pltpu.get_barrier_semaphore()
-    for _, _, to in plan:
-        pl.semaphore_signal(barrier, inc=1, device_id=to, device_id_type=MESH)
-    pl.semaphore_wait(barrier, len(plan))
     copies = []
-    for i, (src, dst, to) in enumerate(plan):
+    for i, (src, dst, to, goes, comes) in enumerate(plan):
+
+        @pl.when(goes)
+        def _():
+            pl.semaphore_signal(barrier, inc=1, device_id=to, device_id_type=MESH)
+
         copy = pltpu.make_async_remote_copy(
             src_ref=src, dst_ref=dst, send_sem=send.at[i], recv_sem=recv.at[i],
             device_id=to, device_id_type=MESH,
         )
-        copy.start()
-        copies.append(copy)
-    for copy in copies:
-        copy.wait()
-
-
-def exchange(axes, ident, xw, xe, yn, ys):
-    corner = jax.ShapeDtypeStruct(yn.shape[1:], F32)
-    shape = lambda a: jax.ShapeDtypeStruct(a.shape, F32)
+        copies.append((copy, goes, comes))
+    pl.semaphore_wait(barrier, sum(jnp.where(step[3], 1, 0) for step in plan))
+    for copy, goes, _ in copies:
+        pl.when(goes)(copy.start)
+    for copy, goes, comes in copies:
+        pl.when(goes)(copy.wait_send)
+        pl.when(comes)(copy.wait_recv)
+
+
+def exchange(axes, ident, *strips):
     return pl.pallas_call(
         functools.partial(exchange_kernel, axes),
-        out_shape=[shape(xw), shape(xw), shape(yn), shape(yn)] + [corner] * 4,
-        in_specs=[pl.BlockSpec(memory_space=pl.ANY)] * 4,
+        out_shape=[jax.ShapeDtypeStruct(s.shape, F32) for s in strips],
+        in_specs=[pl.BlockSpec(memory_space=pl.ANY)] * 8,
         out_specs=[pl.BlockSpec(memory_space=pl.ANY)] * 8,
         scratch_shapes=[pltpu.SemaphoreType.DMA((8,)), pltpu.SemaphoreType.DMA((8,))],
         compiler_params=pltpu.CompilerParams(collective_id=ident, has_side_effects=True),
         name="neighbour_exchange",
-    )(xw, xe, yn, ys)
+    )(*strips)
 
 
 def lay(a, b, west, east):
@@ -156,13 +172,22 @@
     return first, mid, last
 
 
+def unlay(a, b, c):
+    lane, mid = lane_id(), turn(b, 64)
+    return (
+        jnp.where(lane < SPLIT_AB - HALO, turn(a, -HALO), mid),
+        jnp.where(lane < SPLIT_BC - 131, mid, turn(c, HALO)),
+    )
+
+
 def sweep_kernel(axes, steps, rows, *refs):
     prev, src = refs[0:2], refs[2:4]
     coef = [refs[4 + 2 * p : 6 + 2 * p] for p in range(COEFS)]
     base = 4 + 2 * COEFS
     from_w, from_e, from_n, from_s, from_nw, from_ne, from_sw, from_se = refs[base : base + 8]
     waves, co, xw, xe, yn, ys = refs[base + 8 : base + 14]
-    ext, cc, gbuf, carry = refs[base + 14 :]
+    corners = refs[base + 14 : base + 18]
+    ext, cc, gbuf, carry, north_rows, south_rows = refs[base + 18 :]
     has_w, has_e, has_n, has_s = position(axes)
     lane, sub = lane_id(), sub_id()
     zero = jnp.zeros((8, LANES), F32)
@@ -190,19 +215,22 @@
         planes1 = masked_coefs([c[1] for c in coef], at, 1, axes, 8 * t)
         for p in range(COEFS):
             put_own(2 * steps + p, t, planes0[p], planes1[p], 2, p)
-    for j in range(HALO):
-        for strip, cw, ce, flag, row in (
-            (from_n, from_nw, from_ne, has_n, j),
-            (from_s, from_sw, from_se, has_s, rows + HALO + j),
-        ):
-            for q in range(2 * steps // 8 + 1):
-                at = pl.ds(8 * q, 8)
-                a = keep(flag, strip[0, j, at, :])
-                b = keep(flag, strip[1, j, at, :])
-                west = keep(jnp.logical_and(flag, has_w), turn(cw[j, at, :], -125))
-                east = keep(jnp.logical_and(flag, has_e), ce[j, at, :])
-                for g, value in enumerate(lay(a, b, west, east)):
-                    ext[g, pl.ds(8 * q * ROWS_L + row, 8, stride=ROWS_L), :] = value
+    for side, (strip, cw, ce, flag, first) in enumerate((
+        (from_n, from_nw, from_ne, has_n, 0),
+        (from_s, from_sw, from_se, has_s, rows + HALO),
+    )):
+        for q, j, at in strip_blocks(steps, 1 - side):
+            a = keep(flag, strip[0, at : at + 8, :])
+            b = keep(flag, strip[1, at : at + 8, :])
+            slot = 4 * (HALO * q + j)
+            west = keep(jnp.logical_and(flag, has_w), turn(cw[...], -slot))
+            east = keep(jnp.logical_and(flag, has_e), turn(ce[...], -slot))
+            for g, value in enumerate(lay(a, b, west, east)):
+                ext[g, pl.ds(8 * q * ROWS_L + first + j, 8, stride=ROWS_L), :] = value
+    for row in (0, rows + 2 * HALO - 1):
+        for q in range(steps // 8, 2 * steps // 8):
+            for g in range(3):
+                ext[g, pl.ds(8 * q * ROWS_L + row, 8, stride=ROWS_L), :] = zero
     for row in range(rows + 2 * HALO, ROWS_L):
         for q in range(2 * steps // 8 + 1):
             for g in range(3):
@@ -317,8 +345,8 @@
             xe[at, :] = jnp.where(group == n, turn(weighted[2][v], 4 * n + 4), xe[at, :])
         for j in range(HALO):
             for g in range(3):
-                yn[g, j, pl.ds(n, 1), :] = weighted[g][1 + j][0:1]
-                ys[g, j, pl.ds(n, 1), :] = weighted[g][3 + j][7:8]
+                north_rows[g, pl.ds(j * steps + n, 1), :] = weighted[g][1 + j][0:1]
+                south_rows[g, pl.ds(j * steps + n, 1), :] = weighted[g][3 + j][7:8]
         return [[now[g][v] * (1.0 / TAU[DEG]) for v in range(VR)] for g in range(3)]
 
     @pl.loop(0, steps)
@@ -332,6 +360,18 @@
             carry[1, v] = jnp.where(lane < SPLIT_BC - 67, left, turn(c, 67))
             carry[2, v] = jnp.where(lane < SPLIT_BC - 134, turn(b, 61), c)
 
+    for side, (rows_of, out) in enumerate(((north_rows, yn), (south_rows, ys))):
+        packs = [zero, zero]
+        for i in range(HALO * steps // 8):
+            at = slice(8 * i, 8 * i + 8)
+            a, b, c = [rows_of[g, at, :] for g in range(3)]
+            out[0, at, :], out[1, at, :] = unlay(a, b, c)
+            packs[0] = jnp.where(group == i, turn(a, 4 * i - 1), packs[0])
+            packs[1] = jnp.where(group == i, turn(c, 4 * i - 124), packs[1])
+        for h in range(2):
+            out[h, HALO * steps : HALO * steps + 8, :] = packs[h]
+            corners[2 * side + h][...] = packs[h]
+
 
 def chebyshev_scales():
     tau = [1.0, SIGMA]
@@ -355,7 +395,7 @@
     src = refs[10:12]
     agg = refs[12]
     settled, coarse = refs[13:15]
-    before, rest = refs[15:]
+    before, rest, north, south = refs[15:]
     has_w, has_e, has_n, has_s = position(axes)
     lane, sub = lane_id(), sub_id()
     tile = lax.axis_index("gx") * axes[1] + lax.axis_index("gy")
@@ -366,10 +406,23 @@
 
     west_lanes = jnp.logical_and(jnp.logical_and(lane >= 2, lane <= 4), has_w)
     east_lanes = jnp.logical_and(jnp.logical_and(lane >= 123, lane <= 125), has_e)
-    top, bottom = jnp.logical_and(sub == 0, has_n), jnp.logical_and(sub == 7, has_s)
 
     def spread(row):
         return jnp.broadcast_to(row, (8, LANES))
+
+    for strip, cw, ce, flag, out in (
+        (from_n, from_nw, from_ne, has_n, north),
+        (from_s, from_sw, from_se, has_s, south),
+    ):
+        for i in range(HALO * steps // 8):
+            at = slice(8 * i, 8 * i + 8)
+            edge = slice(HALO * steps, HALO * steps + 8)
+            west, east = turn(strip[0, edge, :], 1 - 4 * i), turn(strip[1, edge, :], -1 - 4 * i)
+            a, b, c = lay(strip[0, at, :], strip[1, at, :], west, east)
+            a += jnp.where(west_lanes, turn(cw[...], 2 - 4 * i), 0.0)
+            c += jnp.where(east_lanes, turn(ce[...], 123 - 4 * i), 0.0)
+            for g, value in enumerate((a, b, c)):
+                out[g, at, :] = jnp.where(flag, value, 0.0)
 
     @pl.loop(0, steps)
     def _(n):
@@ -384,17 +437,9 @@
                 if g == 2:
                     total += jnp.where(east_lanes, turn(from_e[at, :], 123 - 4 * n + 4 * LANES), 0.0)
                 if 2 <= v <= 4:
-                    one = pl.ds(n, 1)
-                    total += jnp.where(top, spread(from_n[g, v - 2, one, :]), 0.0)
-                    total += jnp.where(bottom, spread(from_s[g, v - 2, one, :]), 0.0)
-                    if g == 0:
-                        for flag, ref in ((top, from_nw), (bottom, from_sw)):
-                            piece = turn(spread(ref[v - 2, one, :]), 2 - 124)
-                            total += jnp.where(jnp.logical_and(flag, west_lanes), piece, 0.0)
-                    if g == 2:
-                        for flag, ref in ((top, from_ne), (bottom, from_se)):
-                            piece = turn(spread(ref[v - 2, one, :]), 123 - 1)
-                            total += jnp.where(jnp.logical_and(flag, east_lanes), piece, 0.0)
+                    one = pl.ds((v - 2) * steps + n, 1)
+                    total += jnp.where(sub == 0, spread(north[g, one, :]), 0.0)
+                    total += jnp.where(sub == 7, spread(south[g, one, :]), 0.0)
                 now[g][v] = total * co[1, g, at, :]
         out = [[None] * VR for _ in range(3)]
         for g in range(3):
@@ -415,10 +460,7 @@
         for v in range(VR):
             at = pl.ds(n * ROWS_L + v, 8, stride=VR)
             for ref, values in ((settled, now), (rest, out)):
-                a, b, c = values[0][v], values[1][v], values[2][v]
-                mid = turn(b, 64)
-                ref[0, at, :] = jnp.where(lane < SPLIT_AB - HALO, turn(a, -HALO), mid)
-                ref[1, at, :] = jnp.where(lane < SPLIT_BC - 131, mid, turn(c, HALO))
+                ref[0, at, :], ref[1, at, :] = unlay(*[value[v] for value in values])
 
     def add_row(row, total):
         rest_at = pl.ds(row + HALO, steps, stride=ROWS_L)
@@ -551,6 +593,8 @@
     steps, rows, cols = prev_wave.shape
     aggs = coarse_inverse.shape[0]
     planes = 2 * steps + 8
+    strip_rows = HALO * planes - steps
+    rim_rows = HALO * steps
     flat = (steps * rows, cols)
     prev, src = prev_wave.reshape(flat), source.reshape(flat)
     coef = (start_state, storage, leakage, cond_east, cond_south, owner_weight)
@@ -574,19 +618,21 @@
 
     strips = local(
         functools.partial(pack_kernel, axes, steps, rows), "halo_pack", fields, field_specs,
-        [(3, rows, LANES)] * 2 + [(cols // LANES, HALO, planes, LANES)] * 2, [],
+        [(3, rows, LANES)] * 2 + [(2, strip_rows, LANES)] * 2 + [(8, LANES)] * 4, [],
     )
     halo = exchange(axes, 0, *strips)
     waves, co, *rims = local(
         functools.partial(sweep_kernel, axes, steps, rows), "local_sweep",
         fields + list(halo), field_specs + [whole(h.shape) for h in halo],
         [(3, steps * ROWS_L, LANES), (9, 3, ROWS_L, LANES)]
-        + [(ROWS_L, LANES)] * 2 + [(3, HALO, steps, LANES)] * 2,
+        + [(ROWS_L, LANES)] * 2 + [(2, rim_rows + 8, LANES)] * 2 + [(8, LANES)] * 4,
         [
             pltpu.VMEM((3, planes * ROWS_L, LANES), F32),
             pltpu.VMEM((8, 3, VR, 8, LANES), F32),
             pltpu.VMEM((3, VR, 8, LANES), F32),
             pltpu.VMEM((3, VR, 8, LANES), F32),
+            pltpu.VMEM((3, rim_rows, LANES), F32),
+            pltpu.VMEM((3, rim_rows, LANES), F32),
         ],
     )
     rim = exchange(axes, 1, *rims)
@@ -596,7 +642,12 @@
         args + [src, src, aggregate],
         [whole(a.shape) for a in args] + halves(flat) + [whole(aggregate.shape)],
         [(2, steps * ROWS_L, LANES), (steps // 2, 2 * aggs)],
-        [pltpu.VMEM((3, VR, 8, LANES), F32), pltpu.VMEM((2, steps * ROWS_L, LANES), F32)],
+        [
+            pltpu.VMEM((3, VR, 8, LANES), F32),
+            pltpu.VMEM((2, steps * ROWS_L, LANES), F32),
+            pltpu.VMEM((3, rim_rows, LANES), F32),
+            pltpu.VMEM((3, rim_rows, LANES), F32),
+        ],
     )
     everyone = gather(axes, 2, coarse)
     out = pl.pallas_call(

time: 122 us -> 107 us (0.88)
  Pallas kernels: 121 us -> 107 us
    pallas_call x2, Pallas kernels: 40.7 us -> 23.4 us  [exchange(): pl.pallas_call(functools.partial(exchange_kernel, axes), out_shape=[jax.S...]
    pallas_call x1, Pallas kernels: 11.1 us -> 12.6 us  [gather(): pl.pallas_call(functools.partial(gather_kernel, axes), out_shape=jax.Shap...]
    pallas_call x3, Pallas kernels: 60.2 us -> 61.6 us  [local(): pl.pallas_call(kernel, grid=(1,), out_shape=[jax.ShapeDtypeStruct(s, F32)...]
where the time goes in v1:
time: 107 us
  Pallas kernels  107 us (100%)
    pallas_call x3, Pallas kernels, local(): pl.pallas_call(kernel, grid=(1,), out_shape=[jax.ShapeDtypeStruct(s, F32)...  61.6 us
    pallas_call x2, Pallas kernels, exchange(): pl.pallas_call(functools.partial(exchange_kernel, axes), out_shape=[jax.S...  23.4 us
    pallas_call x1, Pallas kernels, gather(): pl.pallas_call(functools.partial(gather_kernel, axes), out_shape=jax.Shap...  12.6 us
    pallas_call x1, Pallas kernels, shards(): pl.pallas_call(functools.partial(correct_kernel, axes, steps, rows, aggs)...  9.39 us

profile of v1, /device:TPU:1, one launch (start us, length us, event | category | flops | bytes accessed | tf_op | source)
XLA Modules:
  0.0 106.9 jit_solution(2270938984490109611)
XLA Ops:
  0.0 5.0 %halo_pack.1 = (f32[3,64,128]{2,1,0:T(8,128)}, f32[3,64,128]{2,1,0:T(8,128)}, f32[2,184,128]{2,1,0:T(8,128)}, f32[2,184,128]{2,1,0:T(8,128)}, f32[8,128]{1,0:T(8...) custom-call(f32[2048,256]{1,0:T(8,128)} %bitcast.9, f32[2048,256]{1,0:T(8,128)} %bitcast.10, ...), custom_call_target="tpu_custom_call" | custom-call | tf_op jit(solution)/shard_map/halo_pack/pallas_call | solution.py:608
  5.0 13.7 %neighbour_exchange.2 = (f32[3,64,128]{2,1,0:T(8,128)}, f32[3,64,128]{2,1,0:T(8,128)}, f32[2,184,128]{2,1,0:T(8,128)}, f32[2,184,128]{2,1,0:T(8,128)}, f32[8,128...) custom-call(f32[3,64,128]{2,1,0:T(8,128)} %get-tuple-element.41.xw, ...), custom_call_target="tpu_custom_call" | custom-call | tf_op jit(solution)/shard_map/neighbour_exchange/pallas_call | solution.py:156
  18.7 39.2 %local_sweep.1 = (f32[3,2304,128]{2,1,0:T(8,128)}, f32[9,3,72,128]{3,2,1,0:T(8,128)}, f32[72,128]{1,0:T(8,128)}, f32[72,128]{1,0:T(8,128)}, f32[2,104,128]{2,1,0...) custom-call(f32[2048,256]{1,0:T(8,128)} %bitcast.11, ...), custom_call_target="tpu_custom_call" | custom-call | tf_op jit(solution)/shard_map/local_sweep/pallas_call | solution.py:608
  57.9 9.7 %neighbour_exchange.3 = (f32[72,128]{1,0:T(8,128)}, f32[72,128]{1,0:T(8,128)}, f32[2,104,128]{2,1,0:T(8,128)}, f32[2,104,128]{2,1,0:T(8,128)}, f32[8,128]{1,0:T(...) custom-call(f32[72,128]{1,0:T(8,128)} %get-tuple-element.59.xw, f32[72,128]{1,0:T(8,128)} %get-tuple-element.60.xe, ...), custom_call_target="tpu_custom_call" | custom-call | tf_op jit(solution)/shard_map/neighbour_exchange/pallas_call | solution.py:156
  67.6 17.4 %settle_and_restrict.1 = (f32[2,2304,128]{2,1,0:T(8,128)}, f32[16,128]{1,0:T(8,128)}) custom-call(f32[3,2304,128]{2,1,0:T(8,128)} %get-tuple-element.57.refs_0_, f32[9,3,72,128]{3,2,1,0:T(8,128)} %get-tuple-element.58.refs_1_, f32[72,128]{1,0:T(8,128)} %get-tuple-element.67.refs_2_, f32[72,128]{1,0:T(8,128)} %get-tuple-element.68.refs_3_, ...), custom_call_target="tpu_custom_call" | custom-call | tf_op jit(solution)/shard_map/settle_and_restrict/pallas_call | solution.py:608
  85.0 12.6 %coarse_gather.1.everyone = f32[32,16,128]{2,1,0:T(8,128)} custom-call(f32[16,128]{1,0:T(8,128)} %get-tuple-element.75.own), custom_call_target="tpu_custom_call" | custom-call | tf_op jit(solution)/shard_map/coarse_gather/pallas_call | solution.py:529
  97.6 9.4 %correct.1 = f32[2048,256]{1,0:T(8,128)} custom-call(f32[32,16,128]{2,1,0:T(8,128)} %coarse_gather.1.everyone, f32[64,2048]{1,0:T(8,128)} %inverse.1, s32[64,256]{1,0:T(8,128)} %agg.1, f32[2,2304,128]{2,1,0:T(8,128)} %get-tuple-element.76.settled), custom_call_target="tpu_custom_call" | custom-call | tf_op jit(solution)/shard_map/correct/pallas_call | solution.py:653

commit v2 on v1

--- a/solution.py
+++ b/solution.py
@@ -16,8 +16,7 @@
 COEFS = 6
 DELTA = 0.95
 SIGMA = 1.0 / DELTA
-OFFSETS = (0, 67, 134)
-SPLIT_AB, SPLIT_BC = 98, 164
+GROUPS = 3
 F32 = jnp.float32
 BF16 = jnp.bfloat16
 MESH = pl.DeviceIdType.MESH
@@ -164,20 +163,71 @@
     )(*strips)
 
 
-def lay(a, b, west, east):
+def spread_matrix(cols):
+    shape = (cols, GROUPS * LANES)
+    at = lax.broadcasted_iota(jnp.int32, shape, 1)
+    col = (at % LANES) * GROUPS + at // LANES - HALO
+    return jnp.where(col == lax.broadcasted_iota(jnp.int32, shape, 0), 1.0, 0.0).astype(BF16)
+
+
+def two_terms(values):
+    high = values.astype(BF16)
+    return jnp.concatenate([high, (values - high.astype(F32)).astype(BF16)], 0)
+
+
+def moved(values, matrix, transposed=False):
+    dims = (((1,), (1 if transposed else 0,)), ((), ()))
+    both = lax.dot_general(two_terms(values), matrix, dims, preferred_element_type=F32)
+    return both[: values.shape[0]] + both[values.shape[0] :]
+
+
+def add_halo(parts, west, east, shift):
     lane = lane_id()
-    first = jnp.where(lane < HALO, west, turn(a, HALO))
-    mid = jnp.where(lane < 64, turn(a, 64), turn(b, 64))
-    last = jnp.where(lane >= LANES - HALO, turn(east, LANES - HALO), turn(b, LANES - HALO))
-    return first, mid, last
-
-
-def unlay(a, b, c):
-    lane, mid = lane_id(), turn(b, 64)
+    at_86 = lane == 86
+    far = turn(east, 85 + shift)
     return (
-        jnp.where(lane < SPLIT_AB - HALO, turn(a, -HALO), mid),
-        jnp.where(lane < SPLIT_BC - 131, mid, turn(c, HALO)),
+        jnp.where(lane == 0, turn(west, shift), jnp.where(lane == 87, far, parts[0])),
+        jnp.where(lane == 0, turn(west, shift - 1), jnp.where(at_86, turn(east, 86 + shift), parts[1])),
+        jnp.where(lane == 0, turn(west, shift - 2), jnp.where(at_86, far, parts[2])),
     )
+
+
+def west_edge(parts, to):
+    lane = lane_id()
+    pair = turn(jnp.where(lane == 0, parts[2], parts[0]), to + 1)
+    return jnp.where(lane == to, turn(parts[1], to), pair)
+
+
+def east_edge(parts, to):
+    lane = lane_id()
+    last = jnp.where(lane == to + 1, turn(parts[1], to - 85 + LANES), turn(parts[2], to - 84 + LANES))
+    return jnp.where(lane == to, turn(parts[0], to - 86 + LANES), last)
+
+
+def add_west(parts, strip, shift, flag):
+    lane, out = lane_id(), list(parts)
+    near = jnp.where(flag, turn(strip, shift), 0.0)
+    out[2] += jnp.where(lane == 0, near, 0.0)
+    out[0] += jnp.where(lane == 1, near, 0.0)
+    out[1] += jnp.where(jnp.logical_and(lane == 1, flag), turn(strip, shift - 1), 0.0)
+    return out
+
+
+def add_east(parts, strip, shift, flag):
+    lane, out = lane_id(), list(parts)
+    near = jnp.where(flag, turn(strip, 85 + shift), 0.0)
+    out[2] += jnp.where(lane == 85, near, 0.0)
+    out[0] += jnp.where(lane == 86, near, 0.0)
+    out[1] += jnp.where(jnp.logical_and(lane == 86, flag), turn(strip, 84 + shift), 0.0)
+    return out
+
+
+def neighbours(y, g, v):
+    down = y[g][v + 1] if v < VR - 1 else pltpu.roll(y[g][0], 7, 0)
+    up = y[g][v - 1] if v else pltpu.roll(y[g][VR - 1], 1, 0)
+    east = y[g + 1][v] if g < GROUPS - 1 else turn(y[0][v], LANES - 1)
+    west = y[g - 1][v] if g else turn(y[GROUPS - 1][v], 1)
+    return east, west, down, up
 
 
 def sweep_kernel(axes, steps, rows, *refs):
@@ -195,37 +245,47 @@
     def keep(flag, value):
         return jnp.where(flag, value, 0.0)
 
-    def put_own(plane, t, a, b, k, slot):
+    spreader = spread_matrix(2 * LANES)
+
+    def put_own(plane, t, parts, k, slot):
         at = pl.ds(t * 8, 8)
-        west = keep(has_w, turn(from_w[k, at, :], -4 * slot + LANES * 4))
-        east = keep(has_e, turn(from_e[k, at, :], -4 * slot + LANES * 4))
-        for g, value in enumerate(lay(a, b, west, east)):
+        west, east = keep(has_w, from_w[k, at, :]), keep(has_e, from_e[k, at, :])
+        for g, value in enumerate(add_halo(parts, west, east, 4 * LANES - 4 * slot)):
             ext[g, pl.ds(plane * ROWS_L + HALO + 8 * t, 8), :] = value
 
-    @pl.loop(0, steps)
-    def _(n):
+    def part_of(wide, first):
+        return [wide[first : first + 8, g * LANES : (g + 1) * LANES] for g in range(GROUPS)]
+
+    @pl.loop(0, steps // 4)
+    def _(i):
         for k, arr in enumerate((prev, src)):
-            for t in range(rows // 8):
-                at = pl.ds(pl.multiple_of(n * rows + 8 * t, 8), 8)
-                put_own(k * steps + n, t, arr[0][at, :], arr[1][at, :], k, n)
-
+            at = pl.ds(pl.multiple_of(4 * i * rows, 8), 4 * rows)
+            wide = moved(jnp.concatenate([arr[0][at, :], arr[1][at, :]], 1), spreader)
+            for m in range(4):
+                n = 4 * i + m
+                for t in range(rows // 8):
+                    put_own(k * steps + n, t, part_of(wide, m * rows + 8 * t), k, n)
+
+    lows, highs = [], []
     for t in range(rows // 8):
         at = pl.ds(8 * t, 8)
-        planes0 = masked_coefs([c[0] for c in coef], at, 0, axes, 8 * t)
-        planes1 = masked_coefs([c[1] for c in coef], at, 1, axes, 8 * t)
+        lows += masked_coefs([c[0] for c in coef], at, 0, axes, 8 * t)
+        highs += masked_coefs([c[1] for c in coef], at, 1, axes, 8 * t)
+    wide = jnp.concatenate([jnp.concatenate(lows, 0), jnp.concatenate(highs, 0)], 1)
+    wide = moved(wide, spreader)
+    for t in range(rows // 8):
         for p in range(COEFS):
-            put_own(2 * steps + p, t, planes0[p], planes1[p], 2, p)
+            put_own(2 * steps + p, t, part_of(wide, 8 * (t * COEFS + p)), 2, p)
     for side, (strip, cw, ce, flag, first) in enumerate((
         (from_n, from_nw, from_ne, has_n, 0),
         (from_s, from_sw, from_se, has_s, rows + HALO),
     )):
+        wide = moved(keep(flag, jnp.concatenate([strip[0], strip[1]], 1)), spreader)
+        west = keep(jnp.logical_and(flag, has_w), cw[...])
+        east = keep(jnp.logical_and(flag, has_e), ce[...])
         for q, j, at in strip_blocks(steps, 1 - side):
-            a = keep(flag, strip[0, at : at + 8, :])
-            b = keep(flag, strip[1, at : at + 8, :])
-            slot = 4 * (HALO * q + j)
-            west = keep(jnp.logical_and(flag, has_w), turn(cw[...], -slot))
-            east = keep(jnp.logical_and(flag, has_e), turn(ce[...], -slot))
-            for g, value in enumerate(lay(a, b, west, east)):
+            shift = 4 * LANES - 4 * (HALO * q + j)
+            for g, value in enumerate(add_halo(part_of(wide, at), west, east, shift)):
                 ext[g, pl.ds(8 * q * ROWS_L + first + j, 8, stride=ROWS_L), :] = value
     for row in (0, rows + 2 * HALO - 1):
         for q in range(steps // 8, 2 * steps // 8):
@@ -240,8 +300,9 @@
         return ext[g, pl.ds(index * ROWS_L + v, 8, stride=VR), :]
 
     first_coef = 2 * steps
+    easts = [[plane(2 * steps + 3, v, g) for v in range(VR)] for g in range(3)]
     for g in range(3):
-        col = lane + OFFSETS[g]
+        col = lane * GROUPS + g
         col_in = jnp.logical_and(col >= 1, col <= 260)
         col_own = jnp.logical_and(col >= HALO, col <= 258)
         col_there = jnp.logical_and(
@@ -271,13 +332,13 @@
             start, sto, leak, east, south, owner = [
                 plane(first_coef + p, v, g) for p in range(COEFS)
             ]
-            ea_w = turn(east, 1)
+            ea_w = easts[g - 1][v] if g else turn(easts[GROUPS - 1][v], 1)
             so_n = souths[v - 1] if v else pltpu.roll(souths[VR - 1], 1, 0)
             diag = sto + leak + east + ea_w + south + so_n
             safe = jnp.where(there, diag, 1.0)
             scale = jnp.where(there, 2.0 * SIGMA / safe, 0.0)
-            cc[0, g, v] = jnp.where(lane == LANES - 1, 0.0, scale * east)
-            cc[1, g, v] = jnp.where(lane == 0, 0.0, scale * ea_w)
+            cc[0, g, v] = scale * east
+            cc[1, g, v] = scale * ea_w
             cc[2, g, v] = scale * south
             cc[3, g, v] = scale * so_n
             cc[4, g, v] = scale
@@ -303,14 +364,8 @@
     group = lane // 4
 
     def stencil(y, g, v):
-        cur = y[g][v]
-        down = y[g][v + 1] if v < VR - 1 else pltpu.roll(y[g][0], 7, 0)
-        up = y[g][v - 1] if v else pltpu.roll(y[g][VR - 1], 1, 0)
-        return (
-            cc[0, g, v] * turn(cur, LANES - 1)
-            + cc[1, g, v] * turn(cur, 1)
-            + (cc[2, g, v] * down + cc[3, g, v] * up)
-        )
+        east, west, down, up = neighbours(y, g, v)
+        return (cc[0, g, v] * east + cc[1, g, v] * west) + (cc[2, g, v] * down + cc[3, g, v] * up)
 
     def advance(n, held):
         old = [[None] * VR for _ in range(3)]
@@ -341,8 +396,9 @@
         weighted = [[cc[7, g, v] * now[g][v] for v in range(VR)] for g in range(3)]
         for v in range(VR):
             at = slice(8 * v, 8 * v + 8)
-            xw[at, :] = jnp.where(group == n, turn(weighted[0][v], 4 * n + LANES - 1), xw[at, :])
-            xe[at, :] = jnp.where(group == n, turn(weighted[2][v], 4 * n + 4), xe[at, :])
+            parts = [weighted[g][v] for g in range(GROUPS)]
+            xw[at, :] = jnp.where(group == n, west_edge(parts, 4 * n), xw[at, :])
+            xe[at, :] = jnp.where(group == n, east_edge(parts, 4 * n), xe[at, :])
         for j in range(HALO):
             for g in range(3):
                 north_rows[g, pl.ds(j * steps + n, 1), :] = weighted[g][1 + j][0:1]
@@ -353,24 +409,20 @@
     def _(n):
         held = [[carry[g, v] for v in range(VR)] for g in range(3)]
         held = finish(n, advance(n, held))
-        for v in range(VR):
-            a, b, c = held[0][v], held[1][v], held[2][v]
-            carry[0, v] = jnp.where(lane < SPLIT_AB, a, turn(b, 67))
-            left = jnp.where(lane < SPLIT_AB - 67, turn(a, 61), b)
-            carry[1, v] = jnp.where(lane < SPLIT_BC - 67, left, turn(c, 67))
-            carry[2, v] = jnp.where(lane < SPLIT_BC - 134, turn(b, 61), c)
+        for g in range(GROUPS):
+            for v in range(VR):
+                carry[g, v] = held[g][v]
 
     for side, (rows_of, out) in enumerate(((north_rows, yn), (south_rows, ys))):
-        packs = [zero, zero]
+        west, east = zero, zero
         for i in range(HALO * steps // 8):
             at = slice(8 * i, 8 * i + 8)
-            a, b, c = [rows_of[g, at, :] for g in range(3)]
-            out[0, at, :], out[1, at, :] = unlay(a, b, c)
-            packs[0] = jnp.where(group == i, turn(a, 4 * i - 1), packs[0])
-            packs[1] = jnp.where(group == i, turn(c, 4 * i - 124), packs[1])
-        for h in range(2):
-            out[h, HALO * steps : HALO * steps + 8, :] = packs[h]
-            corners[2 * side + h][...] = packs[h]
+            parts = [rows_of[g, at, :] for g in range(GROUPS)]
+            west = jnp.where(group == i, west_edge(parts, 4 * i), west)
+            east = jnp.where(group == i, east_edge(parts, 4 * i), east)
+        out[...] = rows_of[...]
+        corners[2 * side][...] = west
+        corners[2 * side + 1][...] = east
 
 
 def chebyshev_scales():
@@ -395,7 +447,7 @@
     src = refs[10:12]
     agg = refs[12]
     settled, coarse = refs[13:15]
-    before, rest, north, south = refs[15:]
+    before, both, rest, north, south = refs[15:]
     has_w, has_e, has_n, has_s = position(axes)
     lane, sub = lane_id(), sub_id()
     tile = lax.axis_index("gx") * axes[1] + lax.axis_index("gy")
@@ -404,8 +456,6 @@
         for v in range(VR):
             before[g, v] = co[8, g, 8 * v : 8 * v + 8, :]
 
-    west_lanes = jnp.logical_and(jnp.logical_and(lane >= 2, lane <= 4), has_w)
-    east_lanes = jnp.logical_and(jnp.logical_and(lane >= 123, lane <= 125), has_e)
 
     def spread(row):
         return jnp.broadcast_to(row, (8, LANES))
@@ -416,12 +466,10 @@
     ):
         for i in range(HALO * steps // 8):
             at = slice(8 * i, 8 * i + 8)
-            edge = slice(HALO * steps, HALO * steps + 8)
-            west, east = turn(strip[0, edge, :], 1 - 4 * i), turn(strip[1, edge, :], -1 - 4 * i)
-            a, b, c = lay(strip[0, at, :], strip[1, at, :], west, east)
-            a += jnp.where(west_lanes, turn(cw[...], 2 - 4 * i), 0.0)
-            c += jnp.where(east_lanes, turn(ce[...], 123 - 4 * i), 0.0)
-            for g, value in enumerate((a, b, c)):
+            parts = [strip[g, at, :] for g in range(GROUPS)]
+            parts = add_west(parts, cw[...], -4 * i, has_w)
+            parts = add_east(parts, ce[...], -4 * i, has_e)
+            for g, value in enumerate(parts):
                 out[g, at, :] = jnp.where(flag, value, 0.0)
 
     @pl.loop(0, steps)
@@ -429,13 +477,12 @@
         now = [[None] * VR for _ in range(3)]
         for v in range(VR):
             at = slice(8 * v, 8 * v + 8)
-            for g in range(3):
-                here = pl.ds(pl.multiple_of(n * ROWS_L + 8 * v, 8), 8)
-                total = co[0, g, at, :] * waves[g, here, :]
-                if g == 0:
-                    total += jnp.where(west_lanes, turn(from_w[at, :], 2 - 4 * n + 4 * LANES), 0.0)
-                if g == 2:
-                    total += jnp.where(east_lanes, turn(from_e[at, :], 123 - 4 * n + 4 * LANES), 0.0)
+            here = pl.ds(pl.multiple_of(n * ROWS_L + 8 * v, 8), 8)
+            parts = [co[0, g, at, :] * waves[g, here, :] for g in range(GROUPS)]
+            shift = 4 * LANES - 4 * n
+            parts = add_west(parts, from_w[at, :], shift, has_w)
+            parts = add_east(parts, from_e[at, :], shift, has_e)
+            for g, total in enumerate(parts):
                 if 2 <= v <= 4:
                     one = pl.ds((v - 2) * steps + n, 1)
                     total += jnp.where(sub == 0, spread(north[g, one, :]), 0.0)
@@ -446,12 +493,11 @@
             for v in range(VR):
                 at = slice(8 * v, 8 * v + 8)
                 cur = now[g][v]
-                down = now[g][v + 1] if v < VR - 1 else pltpu.roll(now[g][0], 7, 0)
-                up = now[g][v - 1] if v else pltpu.roll(now[g][VR - 1], 1, 0)
+                east, west, down, up = neighbours(now, g, v)
                 image = (
                     co[2, g, at, :] * cur
-                    - co[3, g, at, :] * turn(cur, LANES - 1)
-                    - co[4, g, at, :] * turn(cur, 1)
+                    - co[3, g, at, :] * east
+                    - co[4, g, at, :] * west
                     - co[5, g, at, :] * down
                     - co[6, g, at, :] * up
                 )
@@ -459,19 +505,34 @@
                 before[g, v] = cur
         for v in range(VR):
             at = pl.ds(n * ROWS_L + v, 8, stride=VR)
-            for ref, values in ((settled, now), (rest, out)):
-                ref[0, at, :], ref[1, at, :] = unlay(*[value[v] for value in values])
+            for g in range(GROUPS):
+                both[g, 0, at, :] = now[g][v]
+                both[g, 1, at, :] = out[g][v]
+
+    spreader = spread_matrix(2 * LANES)
+
+    @pl.loop(0, steps // 2)
+    def _(i):
+        pieces = [
+            jnp.concatenate(
+                [both[g, k, pl.ds((2 * i + m) * ROWS_L + HALO, rows), :] for g in range(GROUPS)], 1
+            )
+            for k in range(2)
+            for m in range(2)
+        ]
+        plain = moved(jnp.concatenate(pieces, 0), spreader, transposed=True)
+        at = pl.ds(pl.multiple_of(2 * i * rows, 8), 2 * rows)
+        for h in range(2):
+            lanes = slice(h * LANES, (h + 1) * LANES)
+            settled[h, at, :] = plain[: 2 * rows, lanes]
+            rest[h, at, :] = plain[2 * rows :, lanes] + src[h][at, :]
 
     def add_row(row, total):
-        rest_at = pl.ds(row + HALO, steps, stride=ROWS_L)
-        src_at = pl.ds(row, steps, stride=rows)
-        values = jnp.concatenate([rest[h, rest_at, :] + src[h][src_at, :] for h in range(2)], 1)
-        high = values.astype(BF16)
-        low = (values - high.astype(F32)).astype(BF16)
+        at = pl.ds(row, steps, stride=rows)
+        values = jnp.concatenate([rest[0, at, :], rest[1, at, :]], 1)
         hot = one_hot_of(agg[pl.ds(row, 1), :], aggs, tile * aggs)
         return total + lax.dot_general(
-            jnp.concatenate([high, low], 0), hot, (((1,), (1,)), ((), ())),
-            preferred_element_type=F32,
+            two_terms(values), hot, (((1,), (1,)), ((), ())), preferred_element_type=F32
         )
 
     def add_rows(i, total):
@@ -575,7 +636,7 @@
                 factor, jnp.concatenate([hot, hot], 0), preferred_element_type=F32
             )
             out[pl.ds(row, steps, stride=rows), :] = (
-                settled[0, pl.ds(row + HALO, steps, stride=ROWS_L), :] + grown
+                settled[0, pl.ds(row, steps, stride=rows), :] + grown
             )
 
 
@@ -625,7 +686,7 @@
         functools.partial(sweep_kernel, axes, steps, rows), "local_sweep",
         fields + list(halo), field_specs + [whole(h.shape) for h in halo],
         [(3, steps * ROWS_L, LANES), (9, 3, ROWS_L, LANES)]
-        + [(ROWS_L, LANES)] * 2 + [(2, rim_rows + 8, LANES)] * 2 + [(8, LANES)] * 4,
+        + [(ROWS_L, LANES)] * 2 + [(3, rim_rows, LANES)] * 2 + [(8, LANES)] * 4,
         [
             pltpu.VMEM((3, planes * ROWS_L, LANES), F32),
             pltpu.VMEM((8, 3, VR, 8, LANES), F32),
@@ -641,10 +702,11 @@
         functools.partial(settle_kernel, axes, steps, rows, aggs), "settle_and_restrict",
         args + [src, src, aggregate],
         [whole(a.shape) for a in args] + halves(flat) + [whole(aggregate.shape)],
-        [(2, steps * ROWS_L, LANES), (steps // 2, 2 * aggs)],
+        [(2, steps * rows, LANES), (steps // 2, 2 * aggs)],
         [
             pltpu.VMEM((3, VR, 8, LANES), F32),
-            pltpu.VMEM((2, steps * ROWS_L, LANES), F32),
+            pltpu.VMEM((3, 2, steps * ROWS_L, LANES), F32),
+            pltpu.VMEM((2, steps * rows, LANES), F32),
             pltpu.VMEM((3, rim_rows, LANES), F32),
             pltpu.VMEM((3, rim_rows, LANES), F32),
         ],
@@ -658,7 +720,7 @@
             whole(everyone.shape),
             whole(coarse_inverse.shape),
             pl.BlockSpec((rows, LANES), lambda i: (0, i)),
-            pl.BlockSpec((1, steps * ROWS_L, LANES), lambda i: (i, 0, 0)),
+            pl.BlockSpec((1, steps * rows, LANES), lambda i: (i, 0, 0)),
         ],
         out_specs=pl.BlockSpec((steps * rows, LANES), lambda i: (0, i)),
         scratch_shapes=[pltpu.VMEM((steps, 2 * aggs), BF16)],

time: 107 us -> 106 us (level)
    pallas_call x3, Pallas kernels: 61.6 us -> 58.5 us  [local(): pl.pallas_call(kernel, grid=(1,), out_shape=[jax.ShapeDtypeStruct(s, F32)...]
    pallas_call x2, Pallas kernels: 23.4 us -> 25.1 us  [exchange(): pl.pallas_call(functools.partial(exchange_kernel, axes), out_shape=[jax.S...]
where the time goes in v2:
time: 106 us
  Pallas kernels  106 us (100%)
    pallas_call x3, Pallas kernels, local(): pl.pallas_call(kernel, grid=(1,), out_shape=[jax.ShapeDtypeStruct(s, F32)...  58.5 us
    pallas_call x2, Pallas kernels, exchange(): pl.pallas_call(functools.partial(exchange_kernel, axes), out_shape=[jax.S...  25.1 us
    pallas_call x1, Pallas kernels, gather(): pl.pallas_call(functools.partial(gather_kernel, axes), out_shape=jax.Shap...  12.6 us
    pallas_call x1, Pallas kernels, shards(): pl.pallas_call(functools.partial(correct_kernel, axes, steps, rows, aggs)...  9.57 us

profile of v2, /device:TPU:1, one launch (start us, length us, event | category | flops | bytes accessed | tf_op | source)
XLA Modules:
  0.0 105.8 jit_solution(10481989350361643373)
XLA Ops:
  0.0 5.0 %halo_pack.1 = (f32[3,64,128]{2,1,0:T(8,128)}, f32[3,64,128]{2,1,0:T(8,128)}, f32[2,184,128]{2,1,0:T(8,128)}, f32[2,184,128]{2,1,0:T(8,128)}, f32[8,128]{1,0:T(8...) custom-call(f32[2048,256]{1,0:T(8,128)} %bitcast.9, f32[2048,256]{1,0:T(8,128)} %bitcast.10, ...), custom_call_target="tpu_custom_call" | custom-call | tf_op jit(solution)/shard_map/halo_pack/pallas_call | solution.py:669
  5.0 13.7 %neighbour_exchange.2 = (f32[3,64,128]{2,1,0:T(8,128)}, f32[3,64,128]{2,1,0:T(8,128)}, f32[2,184,128]{2,1,0:T(8,128)}, f32[2,184,128]{2,1,0:T(8,128)}, f32[8,128...) custom-call(f32[3,64,128]{2,1,0:T(8,128)} %get-tuple-element.41.xw, ...), custom_call_target="tpu_custom_call" | custom-call | tf_op jit(solution)/shard_map/neighbour_exchange/pallas_call | solution.py:155
  18.7 34.5 %local_sweep.1 = (f32[3,2304,128]{2,1,0:T(8,128)}, f32[9,3,72,128]{3,2,1,0:T(8,128)}, f32[72,128]{1,0:T(8,128)}, f32[72,128]{1,0:T(8,128)}, f32[3,96,128]{2,1,0:...) custom-call(f32[2048,256]{1,0:T(8,128)} %bitcast.11, ...), custom_call_target="tpu_custom_call" | custom-call | tf_op jit(solution)/shard_map/local_sweep/pallas_call | solution.py:669
  53.2 11.4 %neighbour_exchange.3 = (f32[72,128]{1,0:T(8,128)}, f32[72,128]{1,0:T(8,128)}, f32[3,96,128]{2,1,0:T(8,128)}, f32[3,96,128]{2,1,0:T(8,128)}, f32[8,128]{1,0:T(8,...) custom-call(f32[72,128]{1,0:T(8,128)} %get-tuple-element.59.xw, f32[72,128]{1,0:T(8,128)} %get-tuple-element.60.xe, ...), custom_call_target="tpu_custom_call" | custom-call | tf_op jit(solution)/shard_map/neighbour_exchange/pallas_call | solution.py:155
  64.6 19.0 %settle_and_restrict.1 = (f32[2,2048,128]{2,1,0:T(8,128)}, f32[16,128]{1,0:T(8,128)}) custom-call(f32[3,2304,128]{2,1,0:T(8,128)} %get-tuple-element.57.refs_0_, f32[9,3,72,128]{3,2,1,0:T(8,128)} %get-tuple-element.58.refs_1_, f32[72,128]{1,0:T(8,128)} %get-tuple-element.67.refs_2_, f32[72,128]{1,0:T(8,128)} %get-tuple-element.68.refs_3_, ...), custom_call_target="tpu_custom_call" | custom-call | tf_op jit(solution)/shard_map/settle_and_restrict/pallas_call | solution.py:669
  83.6 12.6 %coarse_gather.1.everyone = f32[32,16,128]{2,1,0:T(8,128)} custom-call(f32[16,128]{1,0:T(8,128)} %get-tuple-element.75.own), custom_call_target="tpu_custom_call" | custom-call | tf_op jit(solution)/shard_map/coarse_gather/pallas_call | solution.py:590
  96.3 9.6 %correct.1 = f32[2048,256]{1,0:T(8,128)} custom-call(f32[32,16,128]{2,1,0:T(8,128)} %coarse_gather.1.everyone, f32[64,2048]{1,0:T(8,128)} %inverse.1, s32[64,256]{1,0:T(8,128)} %agg.1, f32[2,2048,128]{2,1,0:T(8,128)} %get-tuple-element.76.settled), custom_call_target="tpu_custom_call" | custom-call | tf_op jit(solution)/shard_map/correct/pallas_call | solution.py:715

commit v3 on v2

--- a/solution.py
+++ b/solution.py
@@ -368,23 +368,24 @@
         return (cc[0, g, v] * east + cc[1, g, v] * west) + (cc[2, g, v] * down + cc[3, g, v] * up)
 
     def advance(n, held):
-        old = [[None] * VR for _ in range(3)]
-        for g in range(3):
+        def each(value):
+            out = [[None] * VR for _ in range(GROUPS)]
             for v in range(VR):
-                old[g][v] = plane(n, v, g)
+                for g in range(GROUPS):
+                    out[g][v] = value(g, v)
+            return out
+
+        old = each(lambda g, v: plane(n, v, g))
+        for v in range(VR):
+            for g in range(GROUPS):
                 gbuf[g, v] = (
                     cc[4, g, v] * plane(steps + n, v, g)
                     + cc[5, g, v] * held[g][v]
                     + cc[6, g, v] * old[g][v]
                 )
-        now = [
-            [0.5 * (stencil(old, g, v) + gbuf[g, v]) for v in range(VR)] for g in range(3)
-        ]
+        now = each(lambda g, v: 0.5 * (stencil(old, g, v) + gbuf[g, v]))
         for k in range(1, DEG):
-            new = [
-                [stencil(now, g, v) + (TAU[k] * gbuf[g, v] - old[g][v]) for v in range(VR)]
-                for g in range(3)
-            ]
+            new = each(lambda g, v: stencil(now, g, v) + (TAU[k] * gbuf[g, v] - old[g][v]))
             old, now = now, new
         return now
 
@@ -527,60 +528,86 @@
             settled[h, at, :] = plain[: 2 * rows, lanes]
             rest[h, at, :] = plain[2 * rows :, lanes] + src[h][at, :]
 
-    def add_row(row, total):
-        at = pl.ds(row, steps, stride=rows)
-        values = jnp.concatenate([rest[0, at, :], rest[1, at, :]], 1)
-        hot = one_hot_of(agg[pl.ds(row, 1), :], aggs, tile * aggs)
+    def add_rows(i, total):
+        values, hots = [], []
+        for k in range(8):
+            row = 8 * i + k
+            at = pl.ds(row, steps, stride=rows)
+            values += [rest[0, at, :], rest[1, at, :]]
+            hots.append(one_hot_of(agg[pl.ds(row, 1), :], aggs, tile * aggs))
         return total + lax.dot_general(
-            two_terms(values), hot, (((1,), (1,)), ((), ())), preferred_element_type=F32
+            two_terms(jnp.concatenate(values, 1)), jnp.concatenate(hots, 1),
+            (((1,), (1,)), ((), ())), preferred_element_type=F32,
         )
 
-    def add_rows(i, total):
-        for k in range(4):
-            total = add_row(4 * i + k, total)
-        return total
-
-    total = lax.fori_loop(0, rows // 4, add_rows, jnp.zeros((2 * steps, aggs), F32))
+    total = lax.fori_loop(0, rows // 8, add_rows, jnp.zeros((2 * steps, aggs), F32))
     total = total[:steps] + total[steps:]
     coarse[...] = jnp.concatenate([total[: steps // 2], total[steps // 2 :]], 1)
 
 
-def gather_kernel(axes, own, everyone, send, recv, local):
+def gather_kernel(axes, own, everyone, send, recv, pass_send, pass_recv, local):
     n_x, n_y = axes
-    count = n_x * n_y
-    me = lax.axis_index("gx") * n_y + lax.axis_index("gy")
-
-    def other(i):
-        which = lax.rem(me + i, count)
-        return which // n_y, lax.rem(which, n_y)
+    chips = n_x // 2 * n_y
+    gx, gy = lax.axis_index("gx"), lax.axis_index("gy")
+    core = lax.rem(gx, 2)
+    chip = gx // 2 * n_y + gy
+    partner = (gx + 1 - 2 * core, gy)
+
+    def place(which, at_core):
+        x, y = 2 * (which // n_y) + at_core, lax.rem(which, n_y)
+        return (x, y), x * n_y + y
+
+    def step_to(i):
+        return place(lax.rem(chip + i, chips), core)[0]
+
+    def step_from(i, at_core):
+        return place(lax.rem(chip + chips - i, chips), at_core)[1]
 
     barrier = pltpu.get_barrier_semaphore()
 
-    @pl.loop(1, count)
+    @pl.loop(1, chips)
     def _(i):
-        pl.semaphore_signal(barrier, inc=1, device_id=other(i), device_id_type=MESH)
-
-    pl.semaphore_wait(barrier, count - 1)
+        pl.semaphore_signal(barrier, inc=1, device_id=step_to(i), device_id_type=MESH)
+
+    pl.semaphore_signal(barrier, inc=1, device_id=partner, device_id_type=MESH)
+    pl.semaphore_wait(barrier, chips)
+
+    def spread(i, block):
+        return pltpu.make_async_remote_copy(
+            src_ref=own, dst_ref=everyone.at[block], send_sem=send.at[i], recv_sem=recv.at[i],
+            device_id=step_to(i), device_id_type=MESH,
+        )
+
+    def hand_over(i, src, block):
+        return pltpu.make_async_remote_copy(
+            src_ref=src, dst_ref=everyone.at[block], send_sem=pass_send.at[i],
+            recv_sem=pass_recv.at[i], device_id=partner, device_id_type=MESH,
+        )
+
+    me = gx * n_y + gy
     mine = pltpu.make_async_copy(own, everyone.at[me], local)
+
+    @pl.loop(1, chips)
+    def _(i):
+        spread(i, me).start()
+
+    hand_over(0, own, me).start()
     mine.start()
 
-    def copy(i):
-        return pltpu.make_async_remote_copy(
-            src_ref=own, dst_ref=everyone.at[me], send_sem=send.at[i], recv_sem=recv.at[i],
-            device_id=other(i), device_id_type=MESH,
-        )
-
-    @pl.loop(1, count)
+    @pl.loop(1, chips)
     def _(i):
-        copy(i).start()
-
-    @pl.loop(1, count)
+        block = step_from(i, core)
+        spread(i, block).wait_recv()
+        hand_over(i, everyone.at[block], block).start()
+
+    @pl.loop(1, chips)
     def _(i):
-        source = lax.rem(me + count - i, count)
-        pltpu.make_async_remote_copy(
-            src_ref=own, dst_ref=everyone.at[source], send_sem=send.at[i], recv_sem=recv.at[i],
-            device_id=other(i), device_id_type=MESH,
-        ).wait()
+        spread(i, me).wait_send()
+
+    @pl.loop(0, chips)
+    def _(i):
+        hand_over(i, own, me).wait_send()
+        hand_over(i, own, step_from(i, 1 - core)).wait_recv()
 
     mine.wait()
 
@@ -593,8 +620,10 @@
         in_specs=[pl.BlockSpec(memory_space=pl.ANY)],
         out_specs=pl.BlockSpec(memory_space=pl.ANY),
         scratch_shapes=[
-            pltpu.SemaphoreType.DMA((count,)),
-            pltpu.SemaphoreType.DMA((count,)),
+            pltpu.SemaphoreType.DMA((count // 2,)),
+            pltpu.SemaphoreType.DMA((count // 2,)),
+            pltpu.SemaphoreType.DMA((count // 2,)),
+            pltpu.SemaphoreType.DMA((count // 2,)),
             pltpu.SemaphoreType.DMA,
         ],
         compiler_params=pltpu.CompilerParams(collective_id=ident, has_side_effects=True),
@@ -627,17 +656,15 @@
 
     factor = fixed[...]
 
-    @pl.loop(0, rows // 4)
+    @pl.loop(0, rows // 8)
     def _(i):
-        for k in range(4):
-            row = 4 * i + k
-            hot = one_hot_of(agg[pl.ds(row, 1), :], aggs, tile * aggs)
-            grown = jnp.dot(
-                factor, jnp.concatenate([hot, hot], 0), preferred_element_type=F32
-            )
-            out[pl.ds(row, steps, stride=rows), :] = (
-                settled[0, pl.ds(row, steps, stride=rows), :] + grown
-            )
+        hot = jnp.concatenate(
+            [one_hot_of(agg[pl.ds(8 * i + k, 1), :], aggs, tile * aggs) for k in range(8)], 1
+        )
+        grown = jnp.dot(factor, jnp.concatenate([hot, hot], 0), preferred_element_type=F32)
+        for k in range(8):
+            at = pl.ds(8 * i + k, steps, stride=rows)
+            out[at, :] = settled[0, at, :] + grown[:, k * LANES : (k + 1) * LANES]
 
 
 def halves(shape):

time: 106 us -> 98.9 us (0.933)
  Pallas kernels: 106 us -> 98.6 us
    pallas_call x3, Pallas kernels: 58.5 us -> 54.9 us  [local(): pl.pallas_call(kernel, grid=(1,), out_shape=[jax.ShapeDtypeStruct(s, F32)...]
    pallas_call x1, Pallas kernels: 9.57 us -> 7.52 us  [shards(): pl.pallas_call(functools.partial(correct_kernel, axes, steps, rows, aggs)...]
    pallas_call x1, Pallas kernels: 12.6 us -> 11.2 us  [gather(): pl.pallas_call(functools.partial(gather_kernel, axes), out_shape=jax.Shap...]
where the time goes in v3:
time: 98.9 us; the launch traced here: 98.7 us
  Pallas kernels  98.6 us (100%)
    pallas_call x3, Pallas kernels, local(): pl.pallas_call(kernel, grid=(1,), out_shape=[jax.ShapeDtypeStruct(s, F32)...  54.9 us
    pallas_call x2, Pallas kernels, exchange(): pl.pallas_call(functools.partial(exchange_kernel, axes), out_shape=[jax.S...  25.1 us
    pallas_call x1, Pallas kernels, gather(): pl.pallas_call(functools.partial(gather_kernel, axes), out_shape=jax.Shap...  11.2 us
    pallas_call x1, Pallas kernels, shards(): pl.pallas_call(functools.partial(correct_kernel, axes, steps, rows, aggs)...  7.52 us

profile of v3, /device:TPU:1, one launch (start us, length us, event | category | flops | bytes accessed | tf_op | source)
XLA Modules:
  0.0 98.7 jit_solution(9686956162769911846)
XLA Ops:
  0.0 5.0 %halo_pack.1 = (f32[3,64,128]{2,1,0:T(8,128)}, f32[3,64,128]{2,1,0:T(8,128)}, f32[2,184,128]{2,1,0:T(8,128)}, f32[2,184,128]{2,1,0:T(8,128)}, f32[8,128]{1,0:T(8...) custom-call(f32[2048,256]{1,0:T(8,128)} %bitcast.9, f32[2048,256]{1,0:T(8,128)} %bitcast.10, ...), custom_call_target="tpu_custom_call" | custom-call | tf_op jit(solution)/shard_map/halo_pack/pallas_call | solution.py:696
  5.0 13.7 %neighbour_exchange.2 = (f32[3,64,128]{2,1,0:T(8,128)}, f32[3,64,128]{2,1,0:T(8,128)}, f32[2,184,128]{2,1,0:T(8,128)}, f32[2,184,128]{2,1,0:T(8,128)}, f32[8,128...) custom-call(f32[3,64,128]{2,1,0:T(8,128)} %get-tuple-element.41.xw, ...), custom_call_target="tpu_custom_call" | custom-call | tf_op jit(solution)/shard_map/neighbour_exchange/pallas_call | solution.py:155
  18.7 31.8 %local_sweep.1 = (f32[3,2304,128]{2,1,0:T(8,128)}, f32[9,3,72,128]{3,2,1,0:T(8,128)}, f32[72,128]{1,0:T(8,128)}, f32[72,128]{1,0:T(8,128)}, f32[3,96,128]{2,1,0:...) custom-call(f32[2048,256]{1,0:T(8,128)} %bitcast.11, ...), custom_call_target="tpu_custom_call" | custom-call | tf_op jit(solution)/shard_map/local_sweep/pallas_call | solution.py:696
  50.5 11.4 %neighbour_exchange.3 = (f32[72,128]{1,0:T(8,128)}, f32[72,128]{1,0:T(8,128)}, f32[3,96,128]{2,1,0:T(8,128)}, f32[3,96,128]{2,1,0:T(8,128)}, f32[8,128]{1,0:T(8,...) custom-call(f32[72,128]{1,0:T(8,128)} %get-tuple-element.59.xw, f32[72,128]{1,0:T(8,128)} %get-tuple-element.60.xe, ...), custom_call_target="tpu_custom_call" | custom-call | tf_op jit(solution)/shard_map/neighbour_exchange/pallas_call | solution.py:155
  61.9 18.1 %settle_and_restrict.1 = (f32[2,2048,128]{2,1,0:T(8,128)}, f32[16,128]{1,0:T(8,128)}) custom-call(f32[3,2304,128]{2,1,0:T(8,128)} %get-tuple-element.57.refs_0_, f32[9,3,72,128]{3,2,1,0:T(8,128)} %get-tuple-element.58.refs_1_, f32[72,128]{1,0:T(8,128)} %get-tuple-element.67.refs_2_, f32[72,128]{1,0:T(8,128)} %get-tuple-element.68.refs_3_, ...), custom_call_target="tpu_custom_call" | custom-call | tf_op jit(solution)/shard_map/settle_and_restrict/pallas_call | solution.py:696
  80.0 11.2 %coarse_gather.1.everyone = f32[32,16,128]{2,1,0:T(8,128)} custom-call(f32[16,128]{1,0:T(8,128)} %get-tuple-element.75.own), custom_call_target="tpu_custom_call" | custom-call | tf_op jit(solution)/shard_map/coarse_gather/pallas_call | solution.py:617
  91.1 7.5 %correct.1 = f32[2048,256]{1,0:T(8,128)} custom-call(f32[32,16,128]{2,1,0:T(8,128)} %coarse_gather.1.everyone, f32[64,2048]{1,0:T(8,128)} %inverse.1, s32[64,256]{1,0:T(8,128)} %agg.1, f32[2,2048,128]{2,1,0:T(8,128)} %get-tuple-element.76.settled), custom_call_target="tpu_custom_call" | custom-call | tf_op jit(solution)/shard_map/correct/pallas_call | solution.py:742

commit v4 on v3

--- a/solution.py
+++ b/solution.py
@@ -52,10 +52,12 @@
     return start, sto, leak, east, south, owner.astype(F32)
 
 
-def pack_kernel(axes, steps, rows, *refs):
-    prev, src = refs[0:2], refs[2:4]
-    coef = [refs[4 + 2 * p : 6 + 2 * p] for p in range(COEFS)]
-    xw, xe, yn, ys, *corners = refs[4 + 2 * COEFS :]
+def fields_of(refs):
+    return refs[0:2], refs[2:4], [refs[4 + 2 * p : 6 + 2 * p] for p in range(COEFS)]
+
+
+def pack_columns(axes, steps, rows, fields, xw, xe):
+    prev, src, coef = fields
     group = lane_id() // 4
 
     @pl.loop(0, rows // 8)
@@ -81,6 +83,10 @@
         xw[2, at, :] = low
         xe[2, at, :] = high
 
+
+def pack_rows(axes, steps, rows, fields, yn, ys, corners):
+    prev, src, coef = fields
+    group = lane_id() // 4
     for side, (out, first, base) in enumerate(((yn, 0, 0), (ys, rows - HALO, rows - 8))):
         for h in range(2):
             planes = masked_coefs([c[h] for c in coef], pl.ds(base, 8), h, axes, base)
@@ -110,9 +116,8 @@
     return blocks
 
 
-def exchange_kernel(axes, xw, xe, yn, ys, c_nw, c_ne, c_sw, c_se, *refs):
-    outs = refs[:8]
-    send, recv = refs[8:]
+def plan_of(axes, strips, outs, send, recv):
+    xw, xe, yn, ys, c_nw, c_ne, c_sw, c_se = strips
     gx, gy = lax.axis_index("gx"), lax.axis_index("gy")
     has_w, has_e, has_n, has_s = position(axes)
     west, east, north, south = gx - 1, gx + 1, gy - 1, gy + 1
@@ -120,35 +125,83 @@
     has_nw, has_ne = both(has_n, has_w), both(has_n, has_e)
     has_sw, has_se = both(has_s, has_w), both(has_s, has_e)
     from_w, from_e, from_n, from_s, from_nw, from_ne, from_sw, from_se = outs
-    plan = (
+    steps = (
         (yn, from_s, (gx, north), has_n, has_s),
         (ys, from_n, (gx, south), has_s, has_n),
-        (xw, from_e, (west, gy), has_w, has_e),
-        (xe, from_w, (east, gy), has_e, has_w),
         (c_nw, from_se, (west, north), has_nw, has_se),
         (c_ne, from_sw, (east, north), has_ne, has_sw),
         (c_sw, from_ne, (west, south), has_sw, has_ne),
         (c_se, from_nw, (east, south), has_se, has_nw),
+        (xw, from_e, (west, gy), has_w, has_e),
+        (xe, from_w, (east, gy), has_e, has_w),
     )
-    barrier = pltpu.get_barrier_semaphore()
-    copies = []
-    for i, (src, dst, to, goes, comes) in enumerate(plan):
-
-        @pl.when(goes)
-        def _():
-            pl.semaphore_signal(barrier, inc=1, device_id=to, device_id_type=MESH)
-
+    plan = []
+    for i, (src, dst, to, goes, comes) in enumerate(steps):
         copy = pltpu.make_async_remote_copy(
             src_ref=src, dst_ref=dst, send_sem=send.at[i], recv_sem=recv.at[i],
             device_id=to, device_id_type=MESH,
         )
-        copies.append((copy, goes, comes))
-    pl.semaphore_wait(barrier, sum(jnp.where(step[3], 1, 0) for step in plan))
-    for copy, goes, _ in copies:
+        plan.append((copy, to, goes, comes))
+    return plan
+
+
+def greet(plan):
+    barrier = pltpu.get_barrier_semaphore()
+    for _, to, goes, _ in plan:
+
+        @pl.when(goes)
+        def _():
+            pl.semaphore_signal(barrier, inc=1, device_id=to, device_id_type=MESH)
+
+    return lambda: pl.semaphore_wait(barrier, sum(jnp.where(step[2], 1, 0) for step in plan))
+
+
+def start_all(plan):
+    for copy, _, goes, _ in plan:
         pl.when(goes)(copy.start)
-    for copy, goes, comes in copies:
+
+
+def wait_all(plan):
+    for copy, _, goes, comes in plan:
         pl.when(goes)(copy.wait_send)
         pl.when(comes)(copy.wait_recv)
+
+
+def exchange_kernel(axes, *refs):
+    plan = plan_of(axes, refs[:8], refs[8:16], *refs[16:])
+    greet(plan)()
+    start_all(plan)
+    wait_all(plan)
+
+
+def halo_kernel(axes, steps, rows, *refs):
+    count = 4 + 2 * COEFS
+    fields, outs = fields_of(refs[:count]), refs[count : count + 8]
+    strips = refs[count + 8 : count + 16]
+    plan = plan_of(axes, strips, outs, *refs[count + 16 :])
+    all_here = greet(plan)
+    pack_rows(axes, steps, rows, fields, strips[2], strips[3], strips[4:])
+    all_here()
+    start_all(plan[:6])
+    pack_columns(axes, steps, rows, fields, strips[0], strips[1])
+    start_all(plan[6:])
+    wait_all(plan)
+
+
+def halo_exchange(axes, ident, steps, rows, fields, field_specs, shapes):
+    return pl.pallas_call(
+        functools.partial(halo_kernel, axes, steps, rows),
+        grid=(1,),
+        out_shape=[jax.ShapeDtypeStruct(s, F32) for s in shapes],
+        in_specs=field_specs,
+        out_specs=[pl.BlockSpec(memory_space=pl.ANY)] * 8,
+        scratch_shapes=[pltpu.VMEM(s, F32) for s in shapes]
+        + [pltpu.SemaphoreType.DMA((8,)), pltpu.SemaphoreType.DMA((8,))],
+        compiler_params=pltpu.CompilerParams(
+            collective_id=ident, has_side_effects=True, vmem_limit_bytes=VMEM_LIMIT
+        ),
+        name="halo_exchange",
+    )(*fields)
 
 
 def exchange(axes, ident, *strips):
@@ -170,14 +223,20 @@
     return jnp.where(col == lax.broadcasted_iota(jnp.int32, shape, 0), 1.0, 0.0).astype(BF16)
 
 
+def collect_matrix(cols):
+    shape = (GROUPS * LANES, cols)
+    at = lax.broadcasted_iota(jnp.int32, shape, 0)
+    col = (at % LANES) * GROUPS + at // LANES - HALO
+    return jnp.where(col == lax.broadcasted_iota(jnp.int32, shape, 1), 1.0, 0.0).astype(BF16)
+
+
 def two_terms(values):
     high = values.astype(BF16)
     return jnp.concatenate([high, (values - high.astype(F32)).astype(BF16)], 0)
 
 
-def moved(values, matrix, transposed=False):
-    dims = (((1,), (1 if transposed else 0,)), ((), ()))
-    both = lax.dot_general(two_terms(values), matrix, dims, preferred_element_type=F32)
+def moved(values, matrix):
+    both = jnp.dot(two_terms(values), matrix, preferred_element_type=F32)
     return both[: values.shape[0]] + both[values.shape[0] :]
 
 
@@ -414,6 +473,7 @@
             for v in range(VR):
                 carry[g, v] = held[g][v]
 
+    collector = collect_matrix(2 * LANES)
     for side, (rows_of, out) in enumerate(((north_rows, yn), (south_rows, ys))):
         west, east = zero, zero
         for i in range(HALO * steps // 8):
@@ -421,9 +481,11 @@
             parts = [rows_of[g, at, :] for g in range(GROUPS)]
             west = jnp.where(group == i, west_edge(parts, 4 * i), west)
             east = jnp.where(group == i, east_edge(parts, 4 * i), east)
-        out[...] = rows_of[...]
-        corners[2 * side][...] = west
-        corners[2 * side + 1][...] = east
+        plain = moved(jnp.concatenate([rows_of[g] for g in range(GROUPS)], 1), collector)
+        for h, pack in enumerate((west, east)):
+            out[h, : HALO * steps, :] = plain[:, h * LANES : (h + 1) * LANES]
+            out[h, HALO * steps :, :] = pack
+            corners[2 * side + h][...] = pack
 
 
 def chebyshev_scales():
@@ -461,13 +523,19 @@
     def spread(row):
         return jnp.broadcast_to(row, (8, LANES))
 
+    spreader = spread_matrix(2 * LANES)
     for strip, cw, ce, flag, out in (
         (from_n, from_nw, from_ne, has_n, north),
         (from_s, from_sw, from_se, has_s, south),
     ):
-        for i in range(HALO * steps // 8):
+        rim = HALO * steps
+        wide = moved(jnp.concatenate([strip[0, :rim, :], strip[1, :rim, :]], 1), spreader)
+        west, east = strip[0, rim:, :], strip[1, rim:, :]
+        for i in range(rim // 8):
             at = slice(8 * i, 8 * i + 8)
-            parts = [strip[g, at, :] for g in range(GROUPS)]
+            parts = [wide[at, g * LANES : (g + 1) * LANES] for g in range(GROUPS)]
+            parts[2] = jnp.where(lane == 0, turn(west, -1 - 4 * i), parts[2])
+            parts[1] = jnp.where(lane == 86, turn(east, 85 - 4 * i), parts[1])
             parts = add_west(parts, cw[...], -4 * i, has_w)
             parts = add_east(parts, ce[...], -4 * i, has_e)
             for g, value in enumerate(parts):
@@ -510,7 +578,7 @@
                 both[g, 0, at, :] = now[g][v]
                 both[g, 1, at, :] = out[g][v]
 
-    spreader = spread_matrix(2 * LANES)
+    collector = collect_matrix(2 * LANES)
 
     @pl.loop(0, steps // 2)
     def _(i):
@@ -521,7 +589,7 @@
             for k in range(2)
             for m in range(2)
         ]
-        plain = moved(jnp.concatenate(pieces, 0), spreader, transposed=True)
+        plain = moved(jnp.concatenate(pieces, 0), collector)
         at = pl.ds(pl.multiple_of(2 * i * rows, 8), 2 * rows)
         for h in range(2):
             lanes = slice(h * LANES, (h + 1) * LANES)
@@ -704,16 +772,13 @@
             name=name,
         )(*args)
 
-    strips = local(
-        functools.partial(pack_kernel, axes, steps, rows), "halo_pack", fields, field_specs,
-        [(3, rows, LANES)] * 2 + [(2, strip_rows, LANES)] * 2 + [(8, LANES)] * 4, [],
-    )
-    halo = exchange(axes, 0, *strips)
+    shapes = [(3, rows, LANES)] * 2 + [(2, strip_rows, LANES)] * 2 + [(8, LANES)] * 4
+    halo = halo_exchange(axes, 0, steps, rows, fields, field_specs, shapes)
     waves, co, *rims = local(
         functools.partial(sweep_kernel, axes, steps, rows), "local_sweep",
         fields + list(halo), field_specs + [whole(h.shape) for h in halo],
         [(3, steps * ROWS_L, LANES), (9, 3, ROWS_L, LANES)]
-        + [(ROWS_L, LANES)] * 2 + [(3, rim_rows, LANES)] * 2 + [(8, LANES)] * 4,
+        + [(ROWS_L, LANES)] * 2 + [(2, rim_rows + 8, LANES)] * 2 + [(8, LANES)] * 4,
         [
             pltpu.VMEM((3, planes * ROWS_L, LANES), F32),
             pltpu.VMEM((8, 3, VR, 8, LANES), F32),

time: 98.9 us -> 93.9 us (0.949)
  Pallas kernels: 98.6 us -> 93.6 us
    pallas_call x0 -> x1, Pallas kernels: none -> 15.8 us  [halo_exchange(): pl.pallas_call(functools.partial(halo_kernel, axes, steps, rows), grid=(1...]
    pallas_call x2 -> x1, Pallas kernels: 25.1 us -> 9.62 us  [exchange(): pl.pallas_call(functools.partial(exchange_kernel, axes), out_shape=[jax.S...]
    pallas_call x3 -> x2, Pallas kernels: 54.9 us -> 49.5 us  [local(): pl.pallas_call(kernel, grid=(1,), out_shape=[jax.ShapeDtypeStruct(s, F32)...]
where the time goes in v4:
time: 93.9 us; the launch traced here: 93.6 us
  Pallas kernels  93.6 us (100%)
    pallas_call x2, Pallas kernels, local(): pl.pallas_call(kernel, grid=(1,), out_shape=[jax.ShapeDtypeStruct(s, F32)...  49.5 us
    pallas_call x1, Pallas kernels, halo_exchange(): pl.pallas_call(functools.partial(halo_kernel, axes, steps, rows), grid=(1...  15.8 us
    pallas_call x1, Pallas kernels, gather(): pl.pallas_call(functools.partial(gather_kernel, axes), out_shape=jax.Shap...  11.1 us
    pallas_call x1, Pallas kernels, exchange(): pl.pallas_call(functools.partial(exchange_kernel, axes), out_shape=[jax.S...  9.62 us
    pallas_call x1, Pallas kernels, shards(): pl.pallas_call(functools.partial(correct_kernel, axes, steps, rows, aggs)...  7.52 us

profile of v4, /device:TPU:1, one launch (start us, length us, event | category | flops | bytes accessed | tf_op | source)
XLA Modules:
  0.0 93.6 jit_solution(4383798605047854138)
XLA Ops:
  0.0 15.8 %halo_exchange.1 = (f32[3,64,128]{2,1,0:T(8,128)}, f32[3,64,128]{2,1,0:T(8,128)}, f32[2,184,128]{2,1,0:T(8,128)}, f32[2,184,128]{2,1,0:T(8,128)}, f32[8,128]{1,0...) custom-call(f32[2048,256]{1,0:T(8,128)} %bitcast.9, f32[2048,256]{1,0:T(8,128)} %bitcast.10, ...), custom_call_target="tpu_custom_call" | custom-call | tf_op jit(solution)/shard_map/halo_exchange/pallas_call | solution.py:192
  15.8 31.8 %local_sweep.1 = (f32[3,2304,128]{2,1,0:T(8,128)}, f32[9,3,72,128]{3,2,1,0:T(8,128)}, f32[72,128]{1,0:T(8,128)}, f32[72,128]{1,0:T(8,128)}, f32[2,104,128]{2,1,0...) custom-call(f32[2048,256]{1,0:T(8,128)} %bitcast.11, ...), custom_call_target="tpu_custom_call" | custom-call | tf_op jit(solution)/shard_map/local_sweep/pallas_call | solution.py:764
  47.6 9.6 %neighbour_exchange.1 = (f32[72,128]{1,0:T(8,128)}, f32[72,128]{1,0:T(8,128)}, f32[2,104,128]{2,1,0:T(8,128)}, f32[2,104,128]{2,1,0:T(8,128)}, f32[8,128]{1,0:T(...) custom-call(f32[72,128]{1,0:T(8,128)} %get-tuple-element.43.refs_0_, ...), custom_call_target="tpu_custom_call" | custom-call | tf_op jit(solution)/shard_map/neighbour_exchange/pallas_call | solution.py:208
  57.2 17.7 %settle_and_restrict.1 = (f32[2,2048,128]{2,1,0:T(8,128)}, f32[16,128]{1,0:T(8,128)}) custom-call(f32[3,2304,128]{2,1,0:T(8,128)} %get-tuple-element.41.refs_0_, f32[9,3,72,128]{3,2,1,0:T(8,128)} %get-tuple-element.42.refs_1_, f32[72,128]{1,0:T(8,128)} %get-tuple-element.51.refs_2_, f32[72,128]{1,0:T(8,128)} %get-tuple-element.52.refs_3_, ...), custom_call_target="tpu_custom_call" | custom-call | tf_op jit(solution)/shard_map/settle_and_restrict/pallas_call | solution.py:764
  75.0 11.1 %coarse_gather.1.everyone = f32[32,16,128]{2,1,0:T(8,128)} custom-call(f32[16,128]{1,0:T(8,128)} %get-tuple-element.59.own), custom_call_target="tpu_custom_call" | custom-call | tf_op jit(solution)/shard_map/coarse_gather/pallas_call | solution.py:685
  86.1 7.5 %correct.1 = f32[2048,256]{1,0:T(8,128)} custom-call(f32[32,16,128]{2,1,0:T(8,128)} %coarse_gather.1.everyone, f32[64,2048]{1,0:T(8,128)} %inverse.1, s32[64,256]{1,0:T(8,128)} %agg.1, f32[2,2048,128]{2,1,0:T(8,128)} %get-tuple-element.60.settled), custom_call_target="tpu_custom_call" | custom-call | tf_op jit(solution)/shard_map/correct/pallas_call | solution.py:807

commit v5 on v4

--- a/solution.py
+++ b/solution.py
@@ -17,6 +17,7 @@
 DELTA = 0.95
 SIGMA = 1.0 / DELTA
 GROUPS = 3
+CHUNKS = 4
 F32 = jnp.float32
 BF16 = jnp.bfloat16
 MESH = pl.DeviceIdType.MESH
@@ -304,122 +305,128 @@
     def keep(flag, value):
         return jnp.where(flag, value, 0.0)
 
-    spreader = spread_matrix(2 * LANES)
-
-    def put_own(plane, t, parts, k, slot):
-        at = pl.ds(t * 8, 8)
-        west, east = keep(has_w, from_w[k, at, :]), keep(has_e, from_e[k, at, :])
-        for g, value in enumerate(add_halo(parts, west, east, 4 * LANES - 4 * slot)):
-            ext[g, pl.ds(plane * ROWS_L + HALO + 8 * t, 8), :] = value
-
-    def part_of(wide, first):
-        return [wide[first : first + 8, g * LANES : (g + 1) * LANES] for g in range(GROUPS)]
-
-    @pl.loop(0, steps // 4)
-    def _(i):
-        for k, arr in enumerate((prev, src)):
-            at = pl.ds(pl.multiple_of(4 * i * rows, 8), 4 * rows)
-            wide = moved(jnp.concatenate([arr[0][at, :], arr[1][at, :]], 1), spreader)
-            for m in range(4):
-                n = 4 * i + m
-                for t in range(rows // 8):
-                    put_own(k * steps + n, t, part_of(wide, m * rows + 8 * t), k, n)
-
-    lows, highs = [], []
-    for t in range(rows // 8):
-        at = pl.ds(8 * t, 8)
-        lows += masked_coefs([c[0] for c in coef], at, 0, axes, 8 * t)
-        highs += masked_coefs([c[1] for c in coef], at, 1, axes, 8 * t)
-    wide = jnp.concatenate([jnp.concatenate(lows, 0), jnp.concatenate(highs, 0)], 1)
-    wide = moved(wide, spreader)
-    for t in range(rows // 8):
-        for p in range(COEFS):
-            put_own(2 * steps + p, t, part_of(wide, 8 * (t * COEFS + p)), 2, p)
-    for side, (strip, cw, ce, flag, first) in enumerate((
-        (from_n, from_nw, from_ne, has_n, 0),
-        (from_s, from_sw, from_se, has_s, rows + HALO),
-    )):
-        wide = moved(keep(flag, jnp.concatenate([strip[0], strip[1]], 1)), spreader)
-        west = keep(jnp.logical_and(flag, has_w), cw[...])
-        east = keep(jnp.logical_and(flag, has_e), ce[...])
-        for q, j, at in strip_blocks(steps, 1 - side):
-            shift = 4 * LANES - 4 * (HALO * q + j)
-            for g, value in enumerate(add_halo(part_of(wide, at), west, east, shift)):
-                ext[g, pl.ds(8 * q * ROWS_L + first + j, 8, stride=ROWS_L), :] = value
-    for row in (0, rows + 2 * HALO - 1):
-        for q in range(steps // 8, 2 * steps // 8):
-            for g in range(3):
-                ext[g, pl.ds(8 * q * ROWS_L + row, 8, stride=ROWS_L), :] = zero
-    for row in range(rows + 2 * HALO, ROWS_L):
-        for q in range(2 * steps // 8 + 1):
-            for g in range(3):
-                ext[g, pl.ds(8 * q * ROWS_L + row, 8, stride=ROWS_L), :] = zero
-
     def plane(index, v, g):
         return ext[g, pl.ds(index * ROWS_L + v, 8, stride=VR), :]
 
-    first_coef = 2 * steps
-    easts = [[plane(2 * steps + 3, v, g) for v in range(VR)] for g in range(3)]
-    for g in range(3):
-        col = lane * GROUPS + g
-        col_in = jnp.logical_and(col >= 1, col <= 260)
-        col_own = jnp.logical_and(col >= HALO, col <= 258)
-        col_there = jnp.logical_and(
-            jnp.logical_or(col >= HALO, has_w), jnp.logical_or(col <= 258, has_e)
-        )
-        n_cols = (
-            1.0
-            + jnp.where(jnp.logical_and(col <= 4, has_w), 1.0, 0.0)
-            + jnp.where(jnp.logical_and(col >= 257, has_e), 1.0, 0.0)
-        )
-        souths = [plane(first_coef + 4, v, g) for v in range(VR)]
-        for v in range(VR):
-            row = sub * VR + v
-            row_in = jnp.logical_and(row >= 1, row <= 68)
-            row_own = jnp.logical_and(row >= HALO, row <= 66)
-            row_there = jnp.logical_and(
-                jnp.logical_or(row >= HALO, has_n), jnp.logical_or(row <= 66, has_s)
+    chunk = steps // CHUNKS
+    first_step = pl.program_id(0) * chunk
+
+    @pl.when(pl.program_id(0) == 0)
+    def _():
+        spreader = spread_matrix(2 * LANES)
+
+        def put_own(plane, t, parts, k, slot):
+            at = pl.ds(t * 8, 8)
+            west, east = keep(has_w, from_w[k, at, :]), keep(has_e, from_e[k, at, :])
+            for g, value in enumerate(add_halo(parts, west, east, 4 * LANES - 4 * slot)):
+                ext[g, pl.ds(plane * ROWS_L + HALO + 8 * t, 8), :] = value
+
+        def part_of(wide, first):
+            return [wide[first : first + 8, g * LANES : (g + 1) * LANES] for g in range(GROUPS)]
+
+        @pl.loop(0, steps // 4)
+        def _(i):
+            for k, arr in enumerate((prev, src)):
+                at = pl.ds(pl.multiple_of(4 * i * rows, 8), 4 * rows)
+                wide = moved(jnp.concatenate([arr[0][at, :], arr[1][at, :]], 1), spreader)
+                for m in range(4):
+                    n = 4 * i + m
+                    for t in range(rows // 8):
+                        put_own(k * steps + n, t, part_of(wide, m * rows + 8 * t), k, n)
+
+        lows, highs = [], []
+        for t in range(rows // 8):
+            at = pl.ds(8 * t, 8)
+            lows += masked_coefs([c[0] for c in coef], at, 0, axes, 8 * t)
+            highs += masked_coefs([c[1] for c in coef], at, 1, axes, 8 * t)
+        wide = jnp.concatenate([jnp.concatenate(lows, 0), jnp.concatenate(highs, 0)], 1)
+        wide = moved(wide, spreader)
+        for t in range(rows // 8):
+            for p in range(COEFS):
+                put_own(2 * steps + p, t, part_of(wide, 8 * (t * COEFS + p)), 2, p)
+        for side, (strip, cw, ce, flag, first) in enumerate((
+            (from_n, from_nw, from_ne, has_n, 0),
+            (from_s, from_sw, from_se, has_s, rows + HALO),
+        )):
+            wide = moved(keep(flag, jnp.concatenate([strip[0], strip[1]], 1)), spreader)
+            west = keep(jnp.logical_and(flag, has_w), cw[...])
+            east = keep(jnp.logical_and(flag, has_e), ce[...])
+            for q, j, at in strip_blocks(steps, 1 - side):
+                shift = 4 * LANES - 4 * (HALO * q + j)
+                for g, value in enumerate(add_halo(part_of(wide, at), west, east, shift)):
+                    ext[g, pl.ds(8 * q * ROWS_L + first + j, 8, stride=ROWS_L), :] = value
+        for row in (0, rows + 2 * HALO - 1):
+            for q in range(steps // 8, 2 * steps // 8):
+                for g in range(3):
+                    ext[g, pl.ds(8 * q * ROWS_L + row, 8, stride=ROWS_L), :] = zero
+        for row in range(rows + 2 * HALO, ROWS_L):
+            for q in range(2 * steps // 8 + 1):
+                for g in range(3):
+                    ext[g, pl.ds(8 * q * ROWS_L + row, 8, stride=ROWS_L), :] = zero
+
+        first_coef = 2 * steps
+        easts = [[plane(2 * steps + 3, v, g) for v in range(VR)] for g in range(3)]
+        for g in range(3):
+            col = lane * GROUPS + g
+            col_in = jnp.logical_and(col >= 1, col <= 260)
+            col_own = jnp.logical_and(col >= HALO, col <= 258)
+            col_there = jnp.logical_and(
+                jnp.logical_or(col >= HALO, has_w), jnp.logical_or(col <= 258, has_e)
             )
-            inner = jnp.logical_and(row_in, col_in)
-            own = jnp.logical_and(row_own, col_own)
-            there = jnp.logical_and(jnp.logical_and(row_there, col_there), inner)
-            n_rows = (
+            n_cols = (
                 1.0
-                + jnp.where(jnp.logical_and(row <= 4, has_n), 1.0, 0.0)
-                + jnp.where(jnp.logical_and(row >= 65, has_s), 1.0, 0.0)
+                + jnp.where(jnp.logical_and(col <= 4, has_w), 1.0, 0.0)
+                + jnp.where(jnp.logical_and(col >= 257, has_e), 1.0, 0.0)
             )
-            start, sto, leak, east, south, owner = [
-                plane(first_coef + p, v, g) for p in range(COEFS)
-            ]
-            ea_w = easts[g - 1][v] if g else turn(easts[GROUPS - 1][v], 1)
-            so_n = souths[v - 1] if v else pltpu.roll(souths[VR - 1], 1, 0)
-            diag = sto + leak + east + ea_w + south + so_n
-            safe = jnp.where(there, diag, 1.0)
-            scale = jnp.where(there, 2.0 * SIGMA / safe, 0.0)
-            cc[0, g, v] = scale * east
-            cc[1, g, v] = scale * ea_w
-            cc[2, g, v] = scale * south
-            cc[3, g, v] = scale * so_n
-            cc[4, g, v] = scale
-            cc[5, g, v] = scale * sto
-            cc[6, g, v] = jnp.where(inner, 0.0, 2.0 * SIGMA)
-            weight = jnp.where(own, owner, jnp.where(there, 1.0, 0.0))
-            cc[7, g, v] = weight * (1.0 / TAU[DEG])
-            den = jnp.where(there, owner + n_rows * n_cols - 1.0, 1.0)
-            at = slice(8 * v, 8 * v + 8)
-            co[0, g, at, :] = weight
-            co[1, g, at, :] = jnp.where(there, 1.0 / den, 0.0)
-            co[2, g, at, :] = diag
-            co[3, g, at, :] = east
-            co[4, g, at, :] = ea_w
-            co[5, g, at, :] = south
-            co[6, g, at, :] = so_n
-            co[7, g, at, :] = sto
-            co[8, g, at, :] = start
-            carry[g, v] = start
-
-    xw[...] = jnp.zeros_like(xw)
-    xe[...] = jnp.zeros_like(xe)
+            souths = [plane(first_coef + 4, v, g) for v in range(VR)]
+            for v in range(VR):
+                row = sub * VR + v
+                row_in = jnp.logical_and(row >= 1, row <= 68)
+                row_own = jnp.logical_and(row >= HALO, row <= 66)
+                row_there = jnp.logical_and(
+                    jnp.logical_or(row >= HALO, has_n), jnp.logical_or(row <= 66, has_s)
+                )
+                inner = jnp.logical_and(row_in, col_in)
+                own = jnp.logical_and(row_own, col_own)
+                there = jnp.logical_and(jnp.logical_and(row_there, col_there), inner)
+                n_rows = (
+                    1.0
+                    + jnp.where(jnp.logical_and(row <= 4, has_n), 1.0, 0.0)
+                    + jnp.where(jnp.logical_and(row >= 65, has_s), 1.0, 0.0)
+                )
+                start, sto, leak, east, south, owner = [
+                    plane(first_coef + p, v, g) for p in range(COEFS)
+                ]
+                ea_w = easts[g - 1][v] if g else turn(easts[GROUPS - 1][v], 1)
+                so_n = souths[v - 1] if v else pltpu.roll(souths[VR - 1], 1, 0)
+                diag = sto + leak + east + ea_w + south + so_n
+                safe = jnp.where(there, diag, 1.0)
+                scale = jnp.where(there, 2.0 * SIGMA / safe, 0.0)
+                cc[0, g, v] = scale * east
+                cc[1, g, v] = scale * ea_w
+                cc[2, g, v] = scale * south
+                cc[3, g, v] = scale * so_n
+                cc[4, g, v] = scale
+                cc[5, g, v] = scale * sto
+                cc[6, g, v] = jnp.where(inner, 0.0, 2.0 * SIGMA)
+                weight = jnp.where(own, owner, jnp.where(there, 1.0, 0.0))
+                cc[7, g, v] = weight * (1.0 / TAU[DEG])
+                den = jnp.where(there, owner + n_rows * n_cols - 1.0, 1.0)
+                at = slice(8 * v, 8 * v + 8)
+                co[0, g, at, :] = weight
+                co[1, g, at, :] = jnp.where(there, 1.0 / den, 0.0)
+                co[2, g, at, :] = diag
+                co[3, g, at, :] = east
+                co[4, g, at, :] = ea_w
+                co[5, g, at, :] = south
+                co[6, g, at, :] = so_n
+                co[7, g, at, :] = sto
+                co[8, g, at, :] = start
+                carry[g, v] = start
+
+        xw[...] = jnp.zeros_like(xw)
+        xe[...] = jnp.zeros_like(xe)
+
     group = lane // 4
 
     def stencil(y, g, v):
@@ -451,7 +458,7 @@
     def finish(n, now):
         for g in range(3):
             for v in range(VR):
-                at = pl.ds(pl.multiple_of(n * ROWS_L + 8 * v, 8), 8)
+                at = pl.ds(pl.multiple_of((n - first_step) * ROWS_L + 8 * v, 8), 8)
                 waves[g, at, :] = now[g][v] * (1.0 / TAU[DEG])
         weighted = [[cc[7, g, v] * now[g][v] for v in range(VR)] for g in range(3)]
         for v in range(VR):
@@ -465,27 +472,30 @@
                 south_rows[g, pl.ds(j * steps + n, 1), :] = weighted[g][3 + j][7:8]
         return [[now[g][v] * (1.0 / TAU[DEG]) for v in range(VR)] for g in range(3)]
 
-    @pl.loop(0, steps)
-    def _(n):
+    @pl.loop(0, chunk)
+    def _(m):
+        n = first_step + m
         held = [[carry[g, v] for v in range(VR)] for g in range(3)]
         held = finish(n, advance(n, held))
         for g in range(GROUPS):
             for v in range(VR):
                 carry[g, v] = held[g][v]
 
-    collector = collect_matrix(2 * LANES)
-    for side, (rows_of, out) in enumerate(((north_rows, yn), (south_rows, ys))):
-        west, east = zero, zero
-        for i in range(HALO * steps // 8):
-            at = slice(8 * i, 8 * i + 8)
-            parts = [rows_of[g, at, :] for g in range(GROUPS)]
-            west = jnp.where(group == i, west_edge(parts, 4 * i), west)
-            east = jnp.where(group == i, east_edge(parts, 4 * i), east)
-        plain = moved(jnp.concatenate([rows_of[g] for g in range(GROUPS)], 1), collector)
-        for h, pack in enumerate((west, east)):
-            out[h, : HALO * steps, :] = plain[:, h * LANES : (h + 1) * LANES]
-            out[h, HALO * steps :, :] = pack
-            corners[2 * side + h][...] = pack
+    @pl.when(pl.program_id(0) == CHUNKS - 1)
+    def _():
+        collector = collect_matrix(2 * LANES)
+        for side, (rows_of, out) in enumerate(((north_rows, yn), (south_rows, ys))):
+            west, east = zero, zero
+            for i in range(HALO * steps // 8):
+                at = slice(8 * i, 8 * i + 8)
+                parts = [rows_of[g, at, :] for g in range(GROUPS)]
+                west = jnp.where(group == i, west_edge(parts, 4 * i), west)
+                east = jnp.where(group == i, east_edge(parts, 4 * i), east)
+            plain = moved(jnp.concatenate([rows_of[g] for g in range(GROUPS)], 1), collector)
+            for h, pack in enumerate((west, east)):
+                out[h, : HALO * steps, :] = plain[:, h * LANES : (h + 1) * LANES]
+                out[h, HALO * steps :, :] = pack
+                corners[2 * side + h][...] = pack
 
 
 def chebyshev_scales():
@@ -515,38 +525,44 @@
     lane, sub = lane_id(), sub_id()
     tile = lax.axis_index("gx") * axes[1] + lax.axis_index("gy")
 
-    for g in range(3):
-        for v in range(VR):
-            before[g, v] = co[8, g, 8 * v : 8 * v + 8, :]
-
-
     def spread(row):
         return jnp.broadcast_to(row, (8, LANES))
 
-    spreader = spread_matrix(2 * LANES)
-    for strip, cw, ce, flag, out in (
-        (from_n, from_nw, from_ne, has_n, north),
-        (from_s, from_sw, from_se, has_s, south),
-    ):
-        rim = HALO * steps
-        wide = moved(jnp.concatenate([strip[0, :rim, :], strip[1, :rim, :]], 1), spreader)
-        west, east = strip[0, rim:, :], strip[1, rim:, :]
-        for i in range(rim // 8):
-            at = slice(8 * i, 8 * i + 8)
-            parts = [wide[at, g * LANES : (g + 1) * LANES] for g in range(GROUPS)]
-            parts[2] = jnp.where(lane == 0, turn(west, -1 - 4 * i), parts[2])
-            parts[1] = jnp.where(lane == 86, turn(east, 85 - 4 * i), parts[1])
-            parts = add_west(parts, cw[...], -4 * i, has_w)
-            parts = add_east(parts, ce[...], -4 * i, has_e)
-            for g, value in enumerate(parts):
-                out[g, at, :] = jnp.where(flag, value, 0.0)
-
-    @pl.loop(0, steps)
-    def _(n):
+    chunk = steps // CHUNKS
+    first_step = pl.program_id(0) * chunk
+
+    @pl.when(pl.program_id(0) == 0)
+    def _():
+        for g in range(3):
+            for v in range(VR):
+                before[g, v] = co[8, g, 8 * v : 8 * v + 8, :]
+
+
+        spreader = spread_matrix(2 * LANES)
+        for strip, cw, ce, flag, out in (
+            (from_n, from_nw, from_ne, has_n, north),
+            (from_s, from_sw, from_se, has_s, south),
+        ):
+            rim = HALO * steps
+            wide = moved(jnp.concatenate([strip[0, :rim, :], strip[1, :rim, :]], 1), spreader)
+            west, east = strip[0, rim:, :], strip[1, rim:, :]
+            for i in range(rim // 8):
+                at = slice(8 * i, 8 * i + 8)
+                parts = [wide[at, g * LANES : (g + 1) * LANES] for g in range(GROUPS)]
+                parts[2] = jnp.where(lane == 0, turn(west, -1 - 4 * i), parts[2])
+                parts[1] = jnp.where(lane == 86, turn(east, 85 - 4 * i), parts[1])
+                parts = add_west(parts, cw[...], -4 * i, has_w)
+                parts = add_east(parts, ce[...], -4 * i, has_e)
+                for g, value in enumerate(parts):
+                    out[g, at, :] = jnp.where(flag, value, 0.0)
+
+    @pl.loop(0, chunk)
+    def _(m):
+        n = first_step + m
         now = [[None] * VR for _ in range(3)]
         for v in range(VR):
             at = slice(8 * v, 8 * v + 8)
-            here = pl.ds(pl.multiple_of(n * ROWS_L + 8 * v, 8), 8)
+            here = pl.ds(pl.multiple_of(m * ROWS_L + 8 * v, 8), 8)
             parts = [co[0, g, at, :] * waves[g, here, :] for g in range(GROUPS)]
             shift = 4 * LANES - 4 * n
             parts = add_west(parts, from_w[at, :], shift, has_w)
@@ -573,14 +589,14 @@
                 out[g][v] = co[7, g, at, :] * before[g, v] - image
                 before[g, v] = cur
         for v in range(VR):
-            at = pl.ds(n * ROWS_L + v, 8, stride=VR)
+            at = pl.ds(m * ROWS_L + v, 8, stride=VR)
             for g in range(GROUPS):
                 both[g, 0, at, :] = now[g][v]
                 both[g, 1, at, :] = out[g][v]
 
     collector = collect_matrix(2 * LANES)
 
-    @pl.loop(0, steps // 2)
+    @pl.loop(0, chunk // 2)
     def _(i):
         pieces = [
             jnp.concatenate(
@@ -594,23 +610,26 @@
         for h in range(2):
             lanes = slice(h * LANES, (h + 1) * LANES)
             settled[h, at, :] = plain[: 2 * rows, lanes]
-            rest[h, at, :] = plain[2 * rows :, lanes] + src[h][at, :]
-
-    def add_rows(i, total):
-        values, hots = [], []
-        for k in range(8):
-            row = 8 * i + k
-            at = pl.ds(row, steps, stride=rows)
-            values += [rest[0, at, :], rest[1, at, :]]
-            hots.append(one_hot_of(agg[pl.ds(row, 1), :], aggs, tile * aggs))
-        return total + lax.dot_general(
-            two_terms(jnp.concatenate(values, 1)), jnp.concatenate(hots, 1),
-            (((1,), (1,)), ((), ())), preferred_element_type=F32,
-        )
-
-    total = lax.fori_loop(0, rows // 8, add_rows, jnp.zeros((2 * steps, aggs), F32))
-    total = total[:steps] + total[steps:]
-    coarse[...] = jnp.concatenate([total[: steps // 2], total[steps // 2 :]], 1)
+            there = pl.ds(pl.multiple_of((first_step + 2 * i) * rows, 8), 2 * rows)
+            rest[h, there, :] = plain[2 * rows :, lanes] + src[h][at, :]
+
+    @pl.when(pl.program_id(0) == CHUNKS - 1)
+    def _():
+        def add_rows(i, total):
+            values, hots = [], []
+            for k in range(8):
+                row = 8 * i + k
+                at = pl.ds(row, steps, stride=rows)
+                values += [rest[0, at, :], rest[1, at, :]]
+                hots.append(one_hot_of(agg[pl.ds(row, 1), :], aggs, tile * aggs))
+            return total + lax.dot_general(
+                two_terms(jnp.concatenate(values, 1)), jnp.concatenate(hots, 1),
+                (((1,), (1,)), ((), ())), preferred_element_type=F32,
+            )
+
+        total = lax.fori_loop(0, rows // 8, add_rows, jnp.zeros((2 * steps, aggs), F32))
+        total = total[:steps] + total[steps:]
+        coarse[...] = jnp.concatenate([total[: steps // 2], total[steps // 2 :]], 1)
 
 
 def gather_kernel(axes, own, everyone, send, recv, pass_send, pass_recv, local):
@@ -760,13 +779,13 @@
         fields += [arr, arr]
         field_specs += halves(arr.shape)
 
-    def local(kernel, name, args, in_specs, outs, scratch):
+    def local(kernel, name, args, in_specs, outs, out_specs, scratch):
         return pl.pallas_call(
             kernel,
-            grid=(1,),
+            grid=(CHUNKS,),
             out_shape=[jax.ShapeDtypeStruct(s, F32) for s in outs],
             in_specs=in_specs,
-            out_specs=[whole(s) for s in outs],
+            out_specs=out_specs + [whole(s) for s in outs[1:]],
             scratch_shapes=scratch,
             compiler_params=params,
             name=name,
@@ -774,11 +793,13 @@
 
     shapes = [(3, rows, LANES)] * 2 + [(2, strip_rows, LANES)] * 2 + [(8, LANES)] * 4
     halo = halo_exchange(axes, 0, steps, rows, fields, field_specs, shapes)
+    wave_spec = pl.BlockSpec((3, steps * ROWS_L // CHUNKS, LANES), lambda i: (0, i, 0))
     waves, co, *rims = local(
         functools.partial(sweep_kernel, axes, steps, rows), "local_sweep",
         fields + list(halo), field_specs + [whole(h.shape) for h in halo],
         [(3, steps * ROWS_L, LANES), (9, 3, ROWS_L, LANES)]
         + [(ROWS_L, LANES)] * 2 + [(2, rim_rows + 8, LANES)] * 2 + [(8, LANES)] * 4,
+        [wave_spec],
         [
             pltpu.VMEM((3, planes * ROWS_L, LANES), F32),
             pltpu.VMEM((8, 3, VR, 8, LANES), F32),
@@ -793,11 +814,18 @@
     settled, coarse = local(
         functools.partial(settle_kernel, axes, steps, rows, aggs), "settle_and_restrict",
         args + [src, src, aggregate],
-        [whole(a.shape) for a in args] + halves(flat) + [whole(aggregate.shape)],
+        [wave_spec]
+        + [whole(a.shape) for a in args[1:]]
+        + [
+            pl.BlockSpec((steps * rows // CHUNKS, LANES), lambda i: (i, 0)),
+            pl.BlockSpec((steps * rows // CHUNKS, LANES), lambda i: (i, 1)),
+            whole(aggregate.shape),
+        ],
         [(2, steps * rows, LANES), (steps // 2, 2 * aggs)],
+        [pl.BlockSpec((2, steps * rows // CHUNKS, LANES), lambda i: (0, i, 0))],
         [
             pltpu.VMEM((3, VR, 8, LANES), F32),
-            pltpu.VMEM((3, 2, steps * ROWS_L, LANES), F32),
+            pltpu.VMEM((3, 2, steps * ROWS_L // CHUNKS, LANES), F32),
             pltpu.VMEM((2, steps * rows, LANES), F32),
             pltpu.VMEM((3, rim_rows, LANES), F32),
             pltpu.VMEM((3, rim_rows, LANES), F32),

time: 93.9 us -> 92.8 us (0.988)
  Pallas kernels: 93.6 us -> 92.5 us
    pallas_call x2, Pallas kernels: 49.5 us -> 48.3 us  [local(): pl.pallas_call(kernel, grid=(CHUNKS,), out_shape=[jax.ShapeDtypeStruct(s,...]
where the time goes in v5:
time: 92.8 us; the launch traced here: 92.5 us
  Pallas kernels  92.5 us (100%)
    pallas_call x2, Pallas kernels, local(): pl.pallas_call(kernel, grid=(CHUNKS,), out_shape=[jax.ShapeDtypeStruct(s,...  48.3 us
    pallas_call x1, Pallas kernels, halo_exchange(): pl.pallas_call(functools.partial(halo_kernel, axes, steps, rows), grid=(1...  15.8 us
    pallas_call x1, Pallas kernels, gather(): pl.pallas_call(functools.partial(gather_kernel, axes), out_shape=jax.Shap...  11.2 us
    pallas_call x1, Pallas kernels, exchange(): pl.pallas_call(functools.partial(exchange_kernel, axes), out_shape=[jax.S...  9.67 us
    pallas_call x1, Pallas kernels, shards(): pl.pallas_call(functools.partial(correct_kernel, axes, steps, rows, aggs)...  7.52 us

profile of v5, /device:TPU:1, one launch (start us, length us, event | category | flops | bytes accessed | tf_op | source)
XLA Modules:
  0.0 92.5 jit_solution(7211721733970118974)
XLA Ops:
  0.0 15.8 %halo_exchange.1 = (f32[3,64,128]{2,1,0:T(8,128)}, f32[3,64,128]{2,1,0:T(8,128)}, f32[2,184,128]{2,1,0:T(8,128)}, f32[2,184,128]{2,1,0:T(8,128)}, f32[8,128]{1,0...) custom-call(f32[2048,256]{1,0:T(8,128)} %bitcast.9, f32[2048,256]{1,0:T(8,128)} %bitcast.10, ...), custom_call_target="tpu_custom_call" | custom-call | tf_op jit(solution)/shard_map/halo_exchange/pallas_call | solution.py:193
  15.8 31.7 %local_sweep.1 = (f32[3,2304,128]{2,1,0:T(8,128)}, f32[9,3,72,128]{3,2,1,0:T(8,128)}, f32[72,128]{1,0:T(8,128)}, f32[72,128]{1,0:T(8,128)}, f32[2,104,128]{2,1,0...) custom-call(f32[2048,256]{1,0:T(8,128)} %bitcast.11, ...), custom_call_target="tpu_custom_call" | custom-call | tf_op jit(solution)/shard_map/local_sweep/pallas_call | solution.py:783
  47.4 9.7 %neighbour_exchange.1 = (f32[72,128]{1,0:T(8,128)}, f32[72,128]{1,0:T(8,128)}, f32[2,104,128]{2,1,0:T(8,128)}, f32[2,104,128]{2,1,0:T(8,128)}, f32[8,128]{1,0:T(...) custom-call(f32[72,128]{1,0:T(8,128)} %get-tuple-element.43.refs_0_, ...), custom_call_target="tpu_custom_call" | custom-call | tf_op jit(solution)/shard_map/neighbour_exchange/pallas_call | solution.py:209
  57.1 16.6 %settle_and_restrict.1 = (f32[2,2048,128]{2,1,0:T(8,128)}, f32[16,128]{1,0:T(8,128)}) custom-call(f32[3,2304,128]{2,1,0:T(8,128)} %get-tuple-element.41.refs_0_, f32[9,3,72,128]{3,2,1,0:T(8,128)} %get-tuple-element.42.refs_1_, f32[72,128]{1,0:T(8,128)} %get-tuple-element.51.refs_2_, f32[72,128]{1,0:T(8,128)} %get-tuple-element.52.refs_3_, ...), custom_call_target="tpu_custom_call" | custom-call | tf_op jit(solution)/shard_map/settle_and_restrict/pallas_call | solution.py:783
  73.8 11.2 %coarse_gather.1.everyone = f32[32,16,128]{2,1,0:T(8,128)} custom-call(f32[16,128]{1,0:T(8,128)} %get-tuple-element.59.own), custom_call_target="tpu_custom_call" | custom-call | tf_op jit(solution)/shard_map/coarse_gather/pallas_call | solution.py:704
  85.0 7.5 %correct.1 = f32[2048,256]{1,0:T(8,128)} custom-call(f32[32,16,128]{2,1,0:T(8,128)} %coarse_gather.1.everyone, f32[64,2048]{1,0:T(8,128)} %inverse.1, s32[64,256]{1,0:T(8,128)} %agg.1, f32[2,2048,128]{2,1,0:T(8,128)} %get-tuple-element.60.settled), custom_call_target="tpu_custom_call" | custom-call | tf_op jit(solution)/shard_map/correct/pallas_call | solution.py:835
